TPU v7x, 128 devices: a whole 4x4x4 slice. The times are simulated.
128 devices in a mesh: chain: 8 (over x, core), band: 16 (over z, y).
Axes of the slice: x: 4, y: 4, z: 4, core: 2. Of those that a mesh axis runs over, the one named last changes fastest.
Arguments:
- diag_inverse: float32 [16384, 2048], P(('chain', 'band'))
- coupling: float32 [16384, 2048], P('chain', 'band'), may hold values from -0.09375 to 0.09375
- elem_stiff: float32 [24, 24, 65536], P(None, None, ('chain', 'band')), may hold values from -6 to 6
- elem_mass: float32 [24, 24, 65536], P(None, None, ('chain', 'band')), may hold values from -6 to 6
- elem_dofs: int32 [24, 65536], P(None, ('chain', 'band')), may hold values from 0 to 2047
- elem_slab: int32 [65536, 1], P(('chain', 'band')), may hold values from 0 to 7; in each aligned block of 512 rows (0 to 511, 512 to 1023, ...) at most 128 rows name the same one
- elem_var: int32 [65536], P(('chain', 'band')), may hold values from 0 to 191
- mode: float32 [16384], P(('chain', 'band')), may hold values from -0.4 to 0.4
- mass_mode: float32 [16384], P('chain'), may hold values from -1.2 to 1.2
- eigenvalue: float32 [1], replicated, may hold values from 0.5 to 2
Outputs:
- eigvec_slope: float32 [192, 16384], P(None, ('chain', 'band'))
- eigval_slope: float32 [192], replicated
Inputs may be any that keep to these rules, and one draw needn't show every extreme that they name: `elem_slab`: within the rows of one device no slab is named by more than 128 elements, a bound that some block reaches.
All inputs are finite; a program needn't handle non-finite values.
Results may differ from a plain program's by a relative error of at most 0.00014.
Values sent between devices are 32-bit elements; how exact they have to be, the bound alone decides.
A program may use at most 64 MiB of HBM per device.

v0:
```python
import jax
import jax.numpy as jnp
from jax import lax
from jax.sharding import PartitionSpec as P

VARS = 192
PANELS = 4


def from_behind(value, axis, by):
    size = lax.axis_size(axis)
    pairs = [(i, i + by) for i in range(size) if 0 <= i + by < size]
    return lax.ppermute(value, axis, pairs)


def sweep(stored, shift_by, iterations, panel_rows, piece_cols, prepare, finish):

    def advance(iteration, carry):
        outgoing, kept = carry
        received = from_behind(outgoing, "chain", shift_by)
        partial_value, context = prepare(iteration, received, kept)
        summed = lax.psum(partial_value, "band")
        return finish(iteration, summed, context, kept)

    outgoing = jnp.zeros((panel_rows, piece_cols), jnp.float32)
    return lax.fori_loop(0, iterations, advance, (outgoing, stored))[1]


def on_device(
    diag_inverse,
    coupling,
    elem_stiff,
    elem_mass,
    elem_dofs,
    elem_slab,
    elem_var,
    mode,
    mass_mode,
    eigenvalue,
):
    highest = lax.Precision.HIGHEST
    chain_len = lax.axis_size("chain")
    chain_pos = lax.axis_index("chain")
    band_pos = lax.axis_index("band")
    piece_cols = diag_inverse.shape[0]
    slab_rows = diag_inverse.shape[1]
    elem_width = elem_dofs.shape[0]
    elem_count = elem_dofs.shape[1]
    capacity = 2 * elem_count // chain_len
    eigen_val = eigenvalue[0]
    whole_mode = lax.all_gather(mode, ("chain", "band"), axis=0, tiled=True)
    dest_slab = elem_slab[:, 0]
    dof_index = dest_slab[None, :] * slab_rows + elem_dofs
    mode_at = whole_mode[dof_index]
    operator = elem_stiff - eigen_val * elem_mass
    loads = -jnp.einsum("ije,je->ie", operator, mode_at, precision=highest)
    quadratic = -jnp.sum(mode_at * loads, axis=0)
    matches = (elem_var[None, :] == jnp.arange(VARS)[:, None]).astype(jnp.float32)
    local_slope = jnp.dot(matches, quadratic, precision=highest)
    eigval_slope = lax.psum(local_slope, ("chain", "band"))
    onehot = (dest_slab[:, None] == jnp.arange(chain_len)[None, :]).astype(jnp.int32)
    slot_rank = jnp.sum((jnp.cumsum(onehot, axis=0) - 1) * onehot, axis=1)
    flat_index = elem_var[None, :] * slab_rows + elem_dofs
    send_values = (
        jnp.zeros((chain_len, elem_width, capacity), jnp.float32)
        .at[dest_slab, :, slot_rank]
        .set(loads.T)
    )
    send_index = (
        jnp.zeros((chain_len, elem_width, capacity), jnp.int32)
        .at[dest_slab, :, slot_rank]
        .set(flat_index.T)
    )
    got_values, got_index = (
        lax.all_to_all(send_values, "chain", split_axis=0, concat_axis=0, tiled=True),
        lax.all_to_all(send_index, "chain", split_axis=0, concat_axis=0, tiled=True),
    )
    assembled = (
        jnp.zeros((VARS * slab_rows,), jnp.float32)
        .at[got_index.reshape(-1)]
        .add(got_values.reshape(-1))
    )
    assembled = assembled.reshape(VARS, slab_rows)
    slope_term = eigval_slope[:, None] * mass_mode[None, :]
    panel_count = PANELS
    panel_rows = VARS // panel_count
    iterations = chain_len + panel_count - 1
    contract = (((1,), (1,)), ((), ()))

    def locate(panel_index):
        active = (panel_index >= 0) & (panel_index < panel_count)
        first_row = jnp.clip(panel_index, 0, panel_count - 1) * panel_rows
        return (active, first_row)

    def place(kept, fresh, active, first_row):
        previous = lax.dynamic_slice_in_dim(kept, first_row, panel_rows, 0)
        return lax.dynamic_update_slice_in_dim(
            kept, jnp.where(active, fresh, previous), first_row, 0
        )

    def forward_prepare(iteration, received, kept):
        active, first_row = locate(iteration - chain_pos)
        rhs_panel = lax.dynamic_slice_in_dim(assembled, first_row, panel_rows, 0)
        carried = lax.dot_general(
            received, coupling, contract, precision=highest, preferred_element_type=jnp.float32
        )
        return (rhs_panel - carried, (active, first_row))

    def forward_finish(iteration, summed, context, kept):
        active, first_row = context
        coupled = summed + lax.dynamic_slice_in_dim(slope_term, first_row, panel_rows, 0)
        fresh = lax.dot_general(
            coupled, diag_inverse, contract, precision=highest, preferred_element_type=jnp.float32
        )
        return (fresh, place(kept, fresh, active, first_row))

    forward_kept = sweep(
        jnp.zeros((VARS, piece_cols), jnp.float32),
        1,
        iterations,
        panel_rows,
        piece_cols,
        forward_prepare,
        forward_finish,
    )

    def backward_prepare(iteration, received, kept):
        active, first_row = locate(iteration - (chain_len - 1 - chain_pos))
        remain = lax.dynamic_slice_in_dim(forward_kept, first_row, panel_rows, 0) - received
        partial_value = jnp.dot(
            remain, diag_inverse, precision=highest, preferred_element_type=jnp.float32
        )
        return (partial_value, (active, first_row))

    def backward_finish(iteration, summed, context, kept):
        active, first_row = context
        own_piece = lax.dynamic_slice_in_dim(summed, band_pos * piece_cols, piece_cols, 1)
        outgoing = jnp.dot(summed, coupling, precision=highest, preferred_element_type=jnp.float32)
        return (outgoing, place(kept, own_piece, active, first_row))

    eigvec_slope = sweep(
        jnp.zeros((VARS, piece_cols), jnp.float32),
        -1,
        iterations,
        panel_rows,
        piece_cols,
        backward_prepare,
        backward_finish,
    )
    return (eigvec_slope, eigval_slope)


def solution(mesh):
    in_specs = (
        P(("chain", "band"), None),
        P("chain", "band"),
        P(None, None, ("chain", "band")),
        P(None, None, ("chain", "band")),
        P(None, ("chain", "band")),
        P(("chain", "band"), None),
        P(("chain", "band")),
        P(("chain", "band")),
        P("chain"),
        P(),
    )
    out_specs = (P(None, ("chain", "band")), P())
    return jax.shard_map(
        on_device, mesh=mesh, in_specs=in_specs, out_specs=out_specs, check_vma=False
    )
```

profile of v0, /device:TPU:0, one launch (start us, length us, event | category | flops | bytes accessed | tf_op | source)
XLA Modules:
  0.0 2479.2 jit_solution(4386069729632127734)
XLA Ops:
  12.4 24.6 scatter_fusion
  37.9 4.3 all-to-all-start
  42.3 47.4 %all-gather = f32[128,1,128]{2,1,0:T(1,128)S(1)} all-gather(f32[1,1,128]{2,1,0:T(1,128)S(1)} %bitcast.64), channel_id=1, replica_groups=mesh['chain'=8,'band'=16] {'chain','band'}, dimensions={0}, use_global_device_ids=true | all-gather | bytes 66048 | tf_op jit(solution)/shard_map/all_gather | solution.py:51
  89.6 68.0 %gather_fusion = f32[12288]{0:T(1024)S(1)} fusion(f32[16384]{0:T(1024)S(1)} %bitcast.50, s32[12288]{0:T(1024)S(1)} %broadcast_clamp_fusion), kind=kCustom, calls=%fused_computation | custom fusion | bytes 147456 | tf_op jit(solution)/shard_map/gather | solution.py:54
  159.1 64.9 %psum.31 = f32[192]{0:T(256)S(1)} all-reduce(f32[192]{0:T(256)S(1)} %bitcast.63), channel_id=1, replica_groups=mesh['chain'=8,'band'=16] {'chain','band'}, use_global_device_ids=true, to_apply=%region_7.8 | all-reduce | flops 192 | bytes 1536 | tf_op jit(solution)/shard_map/psum | solution.py:60
  225.5 24.6 scatter_fusion.1
  250.9 3.4 all-to-all-start.1
  254.4 5.6 all-to-all-done.1
  260.0 129.6 %scatter_custom_fusion.2 = f32[393216]{0:T(1024)} fusion(s32[24576]{0:T(1024)S(1)} %bitcast.57, f32[24576]{0:T(1024)S(1)} %bitcast.56, f32[]{:T(128)} %constant.145.clone.1), kind=kCustom, calls=%fused_computation.17 | custom fusion | flops 24576 | bytes 1572868 | tf_op jit(solution)/shard_map/scatter-add | solution.py:81
  389.6 2.7 reshape.87
  392.3 1066.7 %while.32 = (s32[]{:T(128)}, f32[48,128]{1,0:T(8,128)S(1)}, f32[192,128]{1,0:T(8,128)S(1)}, s32[]{:T(128)}, f32[192,2048]{1,0:T(8,128)}, /*index=5*/f32[2048,128...) while((s32[]{:T(128)}, f32[48,128]{1,0:T(8,128)S(1)}, ...), condition=%wide.region_10.11_spmd, body=%wide.region_8.10_spmd.sunk | while | flops 302290944 | bytes 6227776 | solution.py:26
  392.4 19.7 collective-permute-start
  412.9 2.9 convolution_subtract_fusion.2
  415.9 98.0 %all-reduce.3.cloned.1.call-done = f32[48,2048]{1,0:T(8,128)} async-done(((f32[48,2048]{1,0:T(8,128)}), f32[48,2048]{1,0:T(8,128)}) %all-reduce.3.cloned.1.call-update) | async-done | bytes 393232 | tf_op jit(solution)/shard_map/while/body/eval_jaxpr/psum | solution.py:22
  513.9 2.3 select_dynamic-update-slice_fusion.4
  518.4 2.9 convolution_subtract_fusion.2
  521.4 86.8 %all-reduce.3.cloned.1.call-done = f32[48,2048]{1,0:T(8,128)} async-done(((f32[48,2048]{1,0:T(8,128)}), f32[48,2048]{1,0:T(8,128)}) %all-reduce.3.cloned.1.call-update) | async-done | bytes 393232 | tf_op jit(solution)/shard_map/while/body/eval_jaxpr/psum | solution.py:22
  608.2 2.3 select_dynamic-update-slice_fusion.4
  612.7 2.9 convolution_subtract_fusion.2
  615.7 86.8 %all-reduce.3.cloned.1.call-done = f32[48,2048]{1,0:T(8,128)} async-done(((f32[48,2048]{1,0:T(8,128)}), f32[48,2048]{1,0:T(8,128)}) %all-reduce.3.cloned.1.call-update) | async-done | bytes 393232 | tf_op jit(solution)/shard_map/while/body/eval_jaxpr/psum | solution.py:22
  702.4 2.3 select_dynamic-update-slice_fusion.4
  707.0 2.9 convolution_subtract_fusion.2
  709.9 86.8 %all-reduce.3.cloned.1.call-done = f32[48,2048]{1,0:T(8,128)} async-done(((f32[48,2048]{1,0:T(8,128)}), f32[48,2048]{1,0:T(8,128)}) %all-reduce.3.cloned.1.call-update) | async-done | bytes 393232 | tf_op jit(solution)/shard_map/while/body/eval_jaxpr/psum | solution.py:22
  796.7 2.3 select_dynamic-update-slice_fusion.4
  801.2 2.9 convolution_subtract_fusion.2
  804.2 86.8 %all-reduce.3.cloned.1.call-done = f32[48,2048]{1,0:T(8,128)} async-done(((f32[48,2048]{1,0:T(8,128)}), f32[48,2048]{1,0:T(8,128)}) %all-reduce.3.cloned.1.call-update) | async-done | bytes 393232 | tf_op jit(solution)/shard_map/while/body/eval_jaxpr/psum | solution.py:22
  891.0 2.3 select_dynamic-update-slice_fusion.4
  895.5 2.9 convolution_subtract_fusion.2
  898.5 86.8 %all-reduce.3.cloned.1.call-done = f32[48,2048]{1,0:T(8,128)} async-done(((f32[48,2048]{1,0:T(8,128)}), f32[48,2048]{1,0:T(8,128)}) %all-reduce.3.cloned.1.call-update) | async-done | bytes 393232 | tf_op jit(solution)/shard_map/while/body/eval_jaxpr/psum | solution.py:22
  985.3 2.3 select_dynamic-update-slice_fusion.4
  989.8 2.9 convolution_subtract_fusion.2
  992.8 86.8 %all-reduce.3.cloned.1.call-done = f32[48,2048]{1,0:T(8,128)} async-done(((f32[48,2048]{1,0:T(8,128)}), f32[48,2048]{1,0:T(8,128)}) %all-reduce.3.cloned.1.call-update) | async-done | bytes 393232 | tf_op jit(solution)/shard_map/while/body/eval_jaxpr/psum | solution.py:22
  1079.6 2.3 select_dynamic-update-slice_fusion.4
  1084.1 2.9 convolution_subtract_fusion.2
  1087.1 86.8 %all-reduce.3.cloned.1.call-done = f32[48,2048]{1,0:T(8,128)} async-done(((f32[48,2048]{1,0:T(8,128)}), f32[48,2048]{1,0:T(8,128)}) %all-reduce.3.cloned.1.call-update) | async-done | bytes 393232 | tf_op jit(solution)/shard_map/while/body/eval_jaxpr/psum | solution.py:22
  1173.9 2.3 select_dynamic-update-slice_fusion.4
  1178.4 2.9 convolution_subtract_fusion.2
  1181.4 86.8 %all-reduce.3.cloned.1.call-done = f32[48,2048]{1,0:T(8,128)} async-done(((f32[48,2048]{1,0:T(8,128)}), f32[48,2048]{1,0:T(8,128)}) %all-reduce.3.cloned.1.call-update) | async-done | bytes 393232 | tf_op jit(solution)/shard_map/while/body/eval_jaxpr/psum | solution.py:22
  1268.2 2.3 select_dynamic-update-slice_fusion.4
  1272.7 2.9 convolution_subtract_fusion.2
  1275.6 86.8 %all-reduce.3.cloned.1.call-done = f32[48,2048]{1,0:T(8,128)} async-done(((f32[48,2048]{1,0:T(8,128)}), f32[48,2048]{1,0:T(8,128)}) %all-reduce.3.cloned.1.call-update) | async-done | bytes 393232 | tf_op jit(solution)/shard_map/while/body/eval_jaxpr/psum | solution.py:22
  1362.5 2.3 select_dynamic-update-slice_fusion.4
  1367.0 2.9 convolution_subtract_fusion.2
  1369.9 86.8 %all-reduce.3.cloned.1.call-done = f32[48,2048]{1,0:T(8,128)} async-done(((f32[48,2048]{1,0:T(8,128)}), f32[48,2048]{1,0:T(8,128)}) %all-reduce.3.cloned.1.call-update) | async-done | bytes 393232 | tf_op jit(solution)/shard_map/while/body/eval_jaxpr/psum | solution.py:22
  1456.7 2.3 select_dynamic-update-slice_fusion.4
  1459.1 1012.6 %while.33 = (s32[]{:T(128)}, f32[48,128]{1,0:T(8,128)S(1)}, f32[192,128]{1,0:T(8,128)S(1)}, s32[]{:T(128)}, f32[192,128]{1,0:T(8,128)S(1)}, /*index=5*/f32[128,2...) while((s32[]{:T(128)}, f32[48,128]{1,0:T(8,128)S(1)}, ...), condition=%wide.region_13.14_spmd, body=%wide.region_11.13_spmd.sunk | while | flops 302100480 | bytes 5488969 | solution.py:26
  1460.5 1.8 collective-permute-done.1
  1463.7 85.1 %all-reduce.5.cloned.1.call-done = f32[48,2048]{1,0:T(8,128)} async-done(((f32[48,2048]{1,0:T(8,128)}), f32[48,2048]{1,0:T(8,128)}) %all-reduce.5.cloned.1.call-update) | async-done | bytes 393232 | tf_op jit(solution)/shard_map/while/body/eval_jaxpr/psum | solution.py:22
  1552.5 1.8 collective-permute-done.1
  1555.7 85.1 %all-reduce.5.cloned.1.call-done = f32[48,2048]{1,0:T(8,128)} async-done(((f32[48,2048]{1,0:T(8,128)}), f32[48,2048]{1,0:T(8,128)}) %all-reduce.5.cloned.1.call-update) | async-done | bytes 393232 | tf_op jit(solution)/shard_map/while/body/eval_jaxpr/psum | solution.py:22
  1644.6 1.8 collective-permute-done.1
  1647.8 85.1 %all-reduce.5.cloned.1.call-done = f32[48,2048]{1,0:T(8,128)} async-done(((f32[48,2048]{1,0:T(8,128)}), f32[48,2048]{1,0:T(8,128)}) %all-reduce.5.cloned.1.call-update) | async-done | bytes 393232 | tf_op jit(solution)/shard_map/while/body/eval_jaxpr/psum | solution.py:22
  1736.6 1.8 collective-permute-done.1
  1739.8 85.1 %all-reduce.5.cloned.1.call-done = f32[48,2048]{1,0:T(8,128)} async-done(((f32[48,2048]{1,0:T(8,128)}), f32[48,2048]{1,0:T(8,128)}) %all-reduce.5.cloned.1.call-update) | async-done | bytes 393232 | tf_op jit(solution)/shard_map/while/body/eval_jaxpr/psum | solution.py:22
  1828.7 1.8 collective-permute-done.1
  1831.9 85.1 %all-reduce.5.cloned.1.call-done = f32[48,2048]{1,0:T(8,128)} async-done(((f32[48,2048]{1,0:T(8,128)}), f32[48,2048]{1,0:T(8,128)}) %all-reduce.5.cloned.1.call-update) | async-done | bytes 393232 | tf_op jit(solution)/shard_map/while/body/eval_jaxpr/psum | solution.py:22
  1920.7 1.8 collective-permute-done.1
  1923.9 85.1 %all-reduce.5.cloned.1.call-done = f32[48,2048]{1,0:T(8,128)} async-done(((f32[48,2048]{1,0:T(8,128)}), f32[48,2048]{1,0:T(8,128)}) %all-reduce.5.cloned.1.call-update) | async-done | bytes 393232 | tf_op jit(solution)/shard_map/while/body/eval_jaxpr/psum | solution.py:22
  2012.8 1.8 collective-permute-done.1
  2016.0 85.1 %all-reduce.5.cloned.1.call-done = f32[48,2048]{1,0:T(8,128)} async-done(((f32[48,2048]{1,0:T(8,128)}), f32[48,2048]{1,0:T(8,128)}) %all-reduce.5.cloned.1.call-update) | async-done | bytes 393232 | tf_op jit(solution)/shard_map/while/body/eval_jaxpr/psum | solution.py:22
  2108.0 85.1 %all-reduce.5.cloned.1.call-done = f32[48,2048]{1,0:T(8,128)} async-done(((f32[48,2048]{1,0:T(8,128)}), f32[48,2048]{1,0:T(8,128)}) %all-reduce.5.cloned.1.call-update) | async-done | bytes 393232 | tf_op jit(solution)/shard_map/while/body/eval_jaxpr/psum | solution.py:22
  2200.1 85.1 %all-reduce.5.cloned.1.call-done = f32[48,2048]{1,0:T(8,128)} async-done(((f32[48,2048]{1,0:T(8,128)}), f32[48,2048]{1,0:T(8,128)}) %all-reduce.5.cloned.1.call-update) | async-done | bytes 393232 | tf_op jit(solution)/shard_map/while/body/eval_jaxpr/psum | solution.py:22
  2292.1 85.1 %all-reduce.5.cloned.1.call-done = f32[48,2048]{1,0:T(8,128)} async-done(((f32[48,2048]{1,0:T(8,128)}), f32[48,2048]{1,0:T(8,128)}) %all-reduce.5.cloned.1.call-update) | async-done | bytes 393232 | tf_op jit(solution)/shard_map/while/body/eval_jaxpr/psum | solution.py:22
  2384.2 85.1 %all-reduce.5.cloned.1.call-done = f32[48,2048]{1,0:T(8,128)} async-done(((f32[48,2048]{1,0:T(8,128)}), f32[48,2048]{1,0:T(8,128)}) %all-reduce.5.cloned.1.call-update) | async-done | bytes 393232 | tf_op jit(solution)/shard_map/while/body/eval_jaxpr/psum | solution.py:22
  (161 shorter events, 96.2 us)
Async XLA Ops:
  9.9 32.3 %copy-start.8 = (f32[128]{0:T(128)S(1)}, f32[128]{0:T(128)}, u32[]{:S(2)}) copy-start(f32[128]{0:T(128)} %param.21) | copy-start | bytes 1540
  37.9 213.1 %all-to-all-start = ((s32[8,24,128]{2,1,0:T(8,128)}), s32[8,24,128]{2,1,0:T(8,128)S(1)}, u32[]{:S(2)}, u32[]{:S(2)}) async-start(s32[8,24,128]{2,1,0:T(8,128)} %copy.18), calls=%async_computation | async-start | bytes 196608 | tf_op jit(solution)/shard_map/all_to_all | solution.py:76
  89.6 68.7 %copy-start.2 = (f32[24,24,512]{2,1,0:T(8,128)S(1)}, f32[24,24,512]{2,1,0:T(8,128)}, u32[]{:S(2)}) copy-start(f32[24,24,512]{2,1,0:T(8,128)} %param.16) | copy-start | bytes 3538948
  89.6 68.7 %copy-start.3 = (f32[24,24,512]{2,1,0:T(8,128)S(1)}, f32[24,24,512]{2,1,0:T(8,128)}, u32[]{:S(2)}) copy-start(f32[24,24,512]{2,1,0:T(8,128)} %param.17) | copy-start | bytes 3538948
  157.7 1.1 copy-start.7
  157.7 66.3 %copy-start.5 = (f32[2048]{0:T(1024)S(1)}, f32[2048]{0:T(1024)}, u32[]{:S(2)}) copy-start(f32[2048]{0:T(1024)} %param.22) | copy-start | bytes 24580
  224.0 26.2 %copy-start.6 = (f32[192]{0:T(256)}, f32[192]{0:T(256)S(1)}, u32[]{:S(2)}) copy-start(f32[192]{0:T(256)S(1)} %psum.31) | copy-start | bytes 2308
  250.9 9.1 all-to-all-start.1
  389.6 2.7 copy-start
  389.6 2.7 copy-start.1
  392.3 121.6 %all-reduce.3.cloned.1.call-start = ((), (), s32[]{:S(2)}) async-start(), calls=%async_computation.2 | async-start | bytes 786432 | tf_op jit(solution)/shard_map/while/body/eval_jaxpr/psum | solution.py:22
  392.4 20.6 collective-permute-start
  516.2 92.0 %all-reduce.3.cloned.1.call-start = ((), (), s32[]{:S(2)}) async-start(), calls=%async_computation.2 | async-start | bytes 786432 | tf_op jit(solution)/shard_map/while/body/eval_jaxpr/psum | solution.py:22
  516.3 2.1 collective-permute-start
  610.5 91.9 %all-reduce.3.cloned.1.call-start = ((), (), s32[]{:S(2)}) async-start(), calls=%async_computation.2 | async-start | bytes 786432 | tf_op jit(solution)/shard_map/while/body/eval_jaxpr/psum | solution.py:22
  610.6 2.1 collective-permute-start
  704.8 92.0 %all-reduce.3.cloned.1.call-start = ((), (), s32[]{:S(2)}) async-start(), calls=%async_computation.2 | async-start | bytes 786432 | tf_op jit(solution)/shard_map/while/body/eval_jaxpr/psum | solution.py:22
  704.8 2.1 collective-permute-start
  799.1 92.0 %all-reduce.3.cloned.1.call-start = ((), (), s32[]{:S(2)}) async-start(), calls=%async_computation.2 | async-start | bytes 786432 | tf_op jit(solution)/shard_map/while/body/eval_jaxpr/psum | solution.py:22
  799.1 2.1 collective-permute-start
  893.4 91.9 %all-reduce.3.cloned.1.call-start = ((), (), s32[]{:S(2)}) async-start(), calls=%async_computation.2 | async-start | bytes 786432 | tf_op jit(solution)/shard_map/while/body/eval_jaxpr/psum | solution.py:22
  893.4 2.1 collective-permute-start
  987.6 92.0 %all-reduce.3.cloned.1.call-start = ((), (), s32[]{:S(2)}) async-start(), calls=%async_computation.2 | async-start | bytes 786432 | tf_op jit(solution)/shard_map/while/body/eval_jaxpr/psum | solution.py:22
  987.7 2.1 collective-permute-start
  1081.9 92.0 %all-reduce.3.cloned.1.call-start = ((), (), s32[]{:S(2)}) async-start(), calls=%async_computation.2 | async-start | bytes 786432 | tf_op jit(solution)/shard_map/while/body/eval_jaxpr/psum | solution.py:22
  1082.0 2.1 collective-permute-start
  1176.2 91.9 %all-reduce.3.cloned.1.call-start = ((), (), s32[]{:S(2)}) async-start(), calls=%async_computation.2 | async-start | bytes 786432 | tf_op jit(solution)/shard_map/while/body/eval_jaxpr/psum | solution.py:22
  1176.3 2.1 collective-permute-start
  1270.5 92.0 %all-reduce.3.cloned.1.call-start = ((), (), s32[]{:S(2)}) async-start(), calls=%async_computation.2 | async-start | bytes 786432 | tf_op jit(solution)/shard_map/while/body/eval_jaxpr/psum | solution.py:22
  1270.5 2.1 collective-permute-start
  1364.8 92.0 %all-reduce.3.cloned.1.call-start = ((), (), s32[]{:S(2)}) async-start(), calls=%async_computation.2 | async-start | bytes 786432 | tf_op jit(solution)/shard_map/while/body/eval_jaxpr/psum | solution.py:22
  1364.8 2.1 collective-permute-start
  1459.1 89.7 %all-reduce.5.cloned.1.call-start = ((), (), s32[]{:S(2)}) async-start(), calls=%async_computation.3 | async-start | bytes 786432 | tf_op jit(solution)/shard_map/while/body/eval_jaxpr/psum | solution.py:22
  1459.2 3.1 collective-permute-start.1
  1551.2 89.6 %all-reduce.5.cloned.1.call-start = ((), (), s32[]{:S(2)}) async-start(), calls=%async_computation.3 | async-start | bytes 786432 | tf_op jit(solution)/shard_map/while/body/eval_jaxpr/psum | solution.py:22
  1551.2 3.1 collective-permute-start.1
  1643.3 89.6 %all-reduce.5.cloned.1.call-start = ((), (), s32[]{:S(2)}) async-start(), calls=%async_computation.3 | async-start | bytes 786432 | tf_op jit(solution)/shard_map/while/body/eval_jaxpr/psum | solution.py:22
  1643.3 3.1 collective-permute-start.1
  1735.3 89.6 %all-reduce.5.cloned.1.call-start = ((), (), s32[]{:S(2)}) async-start(), calls=%async_computation.3 | async-start | bytes 786432 | tf_op jit(solution)/shard_map/while/body/eval_jaxpr/psum | solution.py:22
  1735.3 3.1 collective-permute-start.1
  1827.4 89.6 %all-reduce.5.cloned.1.call-start = ((), (), s32[]{:S(2)}) async-start(), calls=%async_computation.3 | async-start | bytes 786432 | tf_op jit(solution)/shard_map/while/body/eval_jaxpr/psum | solution.py:22
  1827.4 3.1 collective-permute-start.1
  1919.4 89.6 %all-reduce.5.cloned.1.call-start = ((), (), s32[]{:S(2)}) async-start(), calls=%async_computation.3 | async-start | bytes 786432 | tf_op jit(solution)/shard_map/while/body/eval_jaxpr/psum | solution.py:22
  1919.4 3.1 collective-permute-start.1
  2011.5 89.6 %all-reduce.5.cloned.1.call-start = ((), (), s32[]{:S(2)}) async-start(), calls=%async_computation.3 | async-start | bytes 786432 | tf_op jit(solution)/shard_map/while/body/eval_jaxpr/psum | solution.py:22
  2011.5 3.1 collective-permute-start.1
  2103.5 89.6 %all-reduce.5.cloned.1.call-start = ((), (), s32[]{:S(2)}) async-start(), calls=%async_computation.3 | async-start | bytes 786432 | tf_op jit(solution)/shard_map/while/body/eval_jaxpr/psum | solution.py:22
  2103.5 3.1 collective-permute-start.1
  2195.5 89.6 %all-reduce.5.cloned.1.call-start = ((), (), s32[]{:S(2)}) async-start(), calls=%async_computation.3 | async-start | bytes 786432 | tf_op jit(solution)/shard_map/while/body/eval_jaxpr/psum | solution.py:22
  2195.6 3.1 collective-permute-start.1
  2287.6 89.6 %all-reduce.5.cloned.1.call-start = ((), (), s32[]{:S(2)}) async-start(), calls=%async_computation.3 | async-start | bytes 786432 | tf_op jit(solution)/shard_map/while/body/eval_jaxpr/psum | solution.py:22
  2287.6 3.1 collective-permute-start.1
  2379.6 89.6 %all-reduce.5.cloned.1.call-start = ((), (), s32[]{:S(2)}) async-start(), calls=%async_computation.3 | async-start | bytes 786432 | tf_op jit(solution)/shard_map/while/body/eval_jaxpr/psum | solution.py:22
  2379.6 3.1 collective-permute-start.1
  2471.7 0.6 copy-start.4
Sparse Core Ops, SparseCore 0:
  416.0 97.8 all-reduce.2
  521.5 86.6 all-reduce.2
  615.8 86.6 all-reduce.2
  710.0 86.6 all-reduce.2
  804.3 86.6 all-reduce.2
  898.6 86.6 all-reduce.2
  992.9 86.6 all-reduce.2
  1087.2 86.6 all-reduce.2
  1181.5 86.6 all-reduce.2
  1275.7 86.6 all-reduce.2
  1370.0 86.6 all-reduce.2
  1463.8 84.9 all-reduce.4
  1555.9 84.9 all-reduce.4
  1647.9 84.9 all-reduce.4
  1740.0 84.9 all-reduce.4
  1832.0 84.9 all-reduce.4
  1924.1 84.9 all-reduce.4
  2016.1 84.9 all-reduce.4
  2108.1 84.9 all-reduce.4
  2200.2 84.9 all-reduce.4
  2292.2 84.9 all-reduce.4
  2384.3 84.9 all-reduce.4
where the time goes:
time: 2480 us
  waiting for transfers between devices  1940 us (78%)
  other arithmetic  145 us (6%)
  local copies, waits for them, and re-layouts  123 us (5%)
  blocking collectives  112 us (5%)
  matrix products  92.1 us (4%)
  starting transfers between devices  54.9 us (2%)
    psum x22, waiting for transfers between devices, advance(): summed = lax.psum(partial_value, 'band')  1900 us
    scatter-add x1, other arithmetic, on_device(): assembled = jnp.zeros((VARS * slab_rows,), jnp.float32).at[got_index.resh...  130 us
    gather x2, local copies, waits for them, and re-layouts, on_device(): mode_at = whole_mode[dof_index]  68 us
    psum x1, blocking collectives, on_device(): eigval_slope = lax.psum(local_slope, ('chain', 'band'))  64.9 us
  transfers between devices with their start and end apart: 46, of which 45 were waited for; matrix products, arithmetic and copies ran while one was open for 4% of the time, Pallas kernels for 0%

commit v1 on v0

v1 whole, which is shorter than its diff:
```python
import functools

import jax
import jax.numpy as jnp
from jax import lax
from jax.experimental import pallas as pl
from jax.experimental.pallas import tpu as pltpu
from jax.sharding import PartitionSpec as P

MESH = pl.DeviceIdType.MESH
F32 = jnp.float32
BF16 = jnp.bfloat16
VARS = 192


def split2(x):
    high = x.astype(BF16)
    return high, (x - high.astype(F32)).astype(BF16)


def stacked_rows(x):
    high = x.astype(BF16).astype(F32)
    return jnp.concatenate([high, x - high], axis=0).astype(BF16)


def sweep_kernel(nc, nb, *refs):
    diag_refs, coup_refs = refs[:nc], refs[nc : 2 * nc]
    (rhs_ref, out_ref, dbuf, cbuf, dsplit, csplit, part, slots, piece, full, ybuf, xbuf,
     load_sem, rs_send, rs_recv, ag_send, ag_recv, out_send, out_recv) = refs[2 * nc :]
    me, band = lax.axis_index("chain"), lax.axis_index("band")
    x_len = nc // 2
    my_x, my_core = me // 2, lax.rem(me, 2)
    rows, width = rhs_ref.shape[1], rhs_ref.shape[2]
    cols = width // nb

    def at_band(b):
        return pl.ds(pl.multiple_of(b * cols, cols), cols)

    for i in range(nc):
        slab = 2 * lax.rem(my_x - i // 2 + x_len, x_len) + lax.rem(my_core + i % 2, 2)
        pltpu.make_async_copy(diag_refs[i], dbuf.at[slab], load_sem.at[0, slab]).start()
        pltpu.make_async_copy(coup_refs[i], cbuf.at[slab], load_sem.at[1, slab]).start()

    barrier = pltpu.get_barrier_semaphore()
    for r in range(1, nb):
        pl.semaphore_signal(barrier, inc=1, device_id=(me, lax.rem(band + r, nb)), device_id_type=MESH)
    for r in range(1, nc):
        pl.semaphore_signal(barrier, inc=1, device_id=(lax.rem(me + r, nc), band), device_id_type=MESH)
    pl.semaphore_wait(barrier, nb + nc - 2)

    def rs_copy(r):
        to = lax.rem(band + r, nb)
        return pltpu.make_async_remote_copy(
            src_ref=part.at[:, at_band(to)], dst_ref=slots.at[r],
            send_sem=rs_send.at[r], recv_sem=rs_recv.at[r], device_id=(me, to), device_id_type=MESH)

    def ag_copy(r):
        to = lax.rem(band + r, nb)
        return pltpu.make_async_remote_copy(
            src_ref=piece, dst_ref=full.at[:, at_band(band)],
            send_sem=ag_send.at[r], recv_sem=ag_recv.at[r], device_id=(me, to), device_id_type=MESH)

    def ag_arrival(r):
        source = lax.rem(band - r + nb, nb)
        return pltpu.make_async_remote_copy(
            src_ref=piece, dst_ref=full.at[:, at_band(source)],
            send_sem=ag_send.at[r], recv_sem=ag_recv.at[r], device_id=(me, source), device_id_type=MESH)

    def reduce_start():
        for r in range(1, nb):
            rs_copy(r).start()

    def reduce_end():
        total = part[:, at_band(band)]
        for r in range(1, nb):
            rs_copy(r).wait_recv()
            total = total + slots[r]
        for r in range(1, nb):
            rs_copy(r).wait_send()
        return total

    def gather_start(value):
        piece[...] = value
        for r in range(1, nb):
            ag_copy(r).start()
        full[:, at_band(band)] = value

    def gather_end():
        for r in range(1, nb):
            ag_arrival(r).wait_recv()
        for r in range(1, nb):
            ag_copy(r).wait_send()

    def split_diag(k):
        pltpu.make_async_copy(diag_refs[0], dbuf.at[k], load_sem.at[0, k]).wait()
        high, low = split2(dbuf[k])
        dsplit[k, 0:cols, :] = high
        dsplit[k, cols : 2 * cols, :] = low

    def split_coup(k):
        pltpu.make_async_copy(coup_refs[0], cbuf.at[k], load_sem.at[1, k]).wait()
        high, low = split2(cbuf[k])
        csplit[k, :, 0:cols] = high
        csplit[k, :, cols : 2 * cols] = low

    nt = (((1,), (1,)), ((), ()))
    nn = (((1,), (0,)), ((), ()))

    def narrow(value, weights, dims):
        wide = lax.dot_general(stacked_rows(value), weights, dims, preferred_element_type=F32)
        return (wide[:rows, :cols] + wide[:rows, cols:]) + (wide[rows:, :cols] + wide[rows:, cols:])

    def spread(value, weights, dims):
        both = stacked_rows(value)
        both = jnp.concatenate([both, both], axis=1)
        wide = lax.dot_general(both, weights, dims, preferred_element_type=F32)
        return wide[:rows] + wide[rows:]

    part[...] = rhs_ref[0]

    def forward(k, carry):
        reduce_start()
        split_diag(k)
        gather_start(reduce_end())

        @pl.when(k + 1 < nc)
        def _():
            split_coup(k + 1)

        gather_end()
        solved = narrow(full[...], dsplit[k], nt)
        ybuf[k] = solved

        @pl.when(k + 1 < nc)
        def _():
            part[...] = rhs_ref[k + 1] - spread(solved, csplit[k + 1], nt)

        return carry

    lax.fori_loop(0, nc, forward, 0)
    split_coup(0)

    def out_copy(k, source):
        return pltpu.make_async_remote_copy(
            src_ref=xbuf.at[k], dst_ref=out_ref.at[pl.ds(pl.multiple_of(source * rows, 8), rows), :],
            send_sem=out_send.at[k], recv_sem=out_recv.at[source], device_id=(k, band), device_id_type=MESH)

    def backward(step, coupled):
        k = nc - 1 - step
        part[...] = spread(ybuf[k] - coupled, dsplit[k], nn)
        reduce_start()
        total = reduce_end()
        gather_start(total)
        xbuf[k] = total

        @pl.when(k != me)
        def _():
            out_copy(k, me).start()

        @pl.when(k == me)
        def _():
            out_ref[pl.ds(pl.multiple_of(me * rows, 8), rows), :] = total

        gather_end()
        return narrow(full[...], csplit[k], nn)

    lax.fori_loop(0, nc, backward, jnp.zeros((rows, cols), F32))

    for r in range(1, nc):
        out_copy(lax.rem(me + r, nc), me).wait_send()
        out_copy(me, lax.rem(me + r, nc)).wait_recv()


def sweep(diag_blocks, coup_blocks, rhs, nc, nb):
    rows, width = rhs.shape[1], rhs.shape[2]
    cols = width // nb
    flops = 2 * nc * 2 * 2 * 2 * (2 * rows) * width * (2 * cols) // 2
    return pl.pallas_call(
        functools.partial(sweep_kernel, nc, nb),
        out_shape=jax.ShapeDtypeStruct((nc * rows, cols), F32),
        in_specs=[pl.BlockSpec(memory_space=pl.ANY)] * (2 * nc) + [pl.BlockSpec(memory_space=pltpu.VMEM)],
        out_specs=pl.BlockSpec(memory_space=pltpu.VMEM),
        scratch_shapes=[
            pltpu.VMEM((nc, cols, width), F32),
            pltpu.VMEM((nc, width, cols), F32),
            pltpu.VMEM((nc, 2 * cols, width), BF16),
            pltpu.VMEM((nc, width, 2 * cols), BF16),
            pltpu.VMEM((rows, width), F32),
            pltpu.VMEM((nb, rows, cols), F32),
            pltpu.VMEM((rows, cols), F32),
            pltpu.VMEM((rows, width), F32),
            pltpu.VMEM((nc, rows, cols), F32),
            pltpu.VMEM((nc, rows, cols), F32),
            pltpu.SemaphoreType.DMA((2, nc)),
            pltpu.SemaphoreType.DMA((nb,)),
            pltpu.SemaphoreType.DMA((nb,)),
            pltpu.SemaphoreType.DMA((nb,)),
            pltpu.SemaphoreType.DMA((nb,)),
            pltpu.SemaphoreType.DMA((nc,)),
            pltpu.SemaphoreType.DMA((nc,)),
        ],
        compiler_params=pltpu.CompilerParams(collective_id=0, has_side_effects=True, vmem_limit_bytes=50 * 1024 * 1024),
        cost_estimate=pl.CostEstimate(flops=flops, bytes_accessed=4 * nc * 2 * cols * width, transcendentals=0),
        name="sweep",
    )(*diag_blocks, *coup_blocks, rhs)


def replicate_chain(block, nc):
    x_len = nc // 2
    found = []
    for by in range(x_len):
        moved = block
        if by:
            pairs = [(2 * x + core, 2 * ((x + by) % x_len) + core) for x in range(x_len) for core in range(2)]
            moved = lax.ppermute(block, "chain", pairs)
        found.append(moved)
    out = []
    swap = [(2 * x + core, 2 * x + 1 - core) for x in range(x_len) for core in range(2)]
    for moved in found:
        out += [moved, lax.ppermute(moved, "chain", swap)]
    return out
def three_way(x):
    high = x.astype(BF16).astype(F32)
    middle = (x - high).astype(BF16).astype(F32)
    return high, middle, x - high - middle


def loads_kernel(nc, nvars, lam_ref, table_ref, stiff_ref, mass_ref, dofs_ref, slab_ref, var_ref,
                 send_ref, slope_ref, mode_at, loads):
    ed, count = dofs_ref.shape
    lanes = table_ref.shape[1]
    cap = send_ref.shape[2]
    per_slab = table_ref.shape[0] // nc
    lam = lam_ref[0]
    dofs, slab, var = dofs_ref[...], slab_ref[...], var_ref[...]
    row_of = slab * per_slab + lax.shift_right_logical(dofs, 7)
    lane_of = jnp.bitwise_and(dofs, lanes - 1)
    chunks = count // lanes

    def look(step, found):
        found = list(found)
        for inner in range(8):
            r = step * 8 + inner
            row = jnp.broadcast_to(table_ref[pl.ds(r, 1), :], (ed, lanes))
            for c in range(chunks):
                at = slice(c * lanes, (c + 1) * lanes)
                taken = jnp.take_along_axis(row, lane_of[:, at], axis=1, mode="promise_in_bounds")
                found[c] = jnp.where(row_of[:, at] == r, taken, found[c])
        return tuple(found)

    found = lax.fori_loop(0, table_ref.shape[0] // 8, look, (jnp.zeros((ed, lanes), F32),) * chunks)
    for c in range(chunks):
        mode_at[:, c * lanes : (c + 1) * lanes] = found[c]
    modes = mode_at[...]
    for i in range(ed):
        operator = stiff_ref[i] - lam * mass_ref[i]
        loads[i : i + 1, :] = -jnp.sum(operator * modes, axis=0, keepdims=True)
    values = loads[...]
    quadratic = -jnp.sum(modes * values, axis=0, keepdims=True)
    matches = (lax.broadcasted_iota(jnp.int32, (nvars, count), 0) == var).astype(F32).astype(BF16)
    terms = jnp.concatenate(list(three_way(quadratic)) + [jnp.zeros((5, count), F32)], axis=0).astype(BF16)
    nt = (((1,), (1,)), ((), ()))
    sums = lax.dot_general(terms, matches, nt, preferred_element_type=F32)
    slope_ref[...] = jnp.sum(sums, axis=0, keepdims=True)
    merged = jnp.zeros((ed, count), F32)
    for i in range(ed):
        merged = merged + jnp.where(dofs == dofs[i : i + 1, :], values[i : i + 1, :], 0.0)
    onehot = (lax.broadcasted_iota(jnp.int32, (nc, count), 0) == slab).astype(F32)
    earlier = lax.broadcasted_iota(jnp.int32, (count, count), 0) < lax.broadcasted_iota(jnp.int32, (count, count), 1)
    rank_all = jnp.dot(onehot.astype(BF16), earlier.astype(F32).astype(BF16), preferred_element_type=F32)
    rank = jnp.sum(onehot * rank_all, axis=0, keepdims=True).astype(jnp.int32)
    slot = slab * cap + rank
    high, middle, low = three_way(merged)
    coarse = lax.shift_right_logical(dofs, 4).astype(F32)
    fine = jnp.bitwise_and(dofs, 15).astype(F32)
    var_rows = jnp.concatenate([var.astype(F32), jnp.zeros((7, count), F32)], axis=0)
    data = jnp.concatenate([high, middle, low, coarse, fine, var_rows], axis=0).astype(BF16)
    for k in range(nc):
        place = (lax.broadcasted_iota(jnp.int32, (cap, count), 0) + k * cap == slot).astype(F32).astype(BF16)
        packed = lax.dot_general(data, place, nt, preferred_element_type=F32)
        send_ref[k, 0:ed, :] = (packed[0:ed] + packed[ed : 2 * ed]) + packed[2 * ed : 3 * ed]
        send_ref[k, ed : 2 * ed, :] = packed[3 * ed : 4 * ed] * 16.0 + packed[4 * ed : 5 * ed]
        send_ref[k, 2 * ed : 2 * ed + 8, :] = packed[5 * ed : 5 * ed + 8]


def scatter_kernel(nc, got_ref, slope_ref, mass_ref, rhs_ref, spread_ref):
    width = mass_ref.shape[1]
    nvars = slope_ref.shape[0]
    cap = got_ref.shape[2]
    ed = (got_ref.shape[1] - 8) // 2
    block = 256
    rows = 128
    base = lax.broadcasted_iota(jnp.int32, (rows, cap), 0)
    variable = lax.broadcasted_iota(jnp.int32, (nvars, cap), 0)
    matches = [(variable == got_ref[s, 2 * ed : 2 * ed + 1, :].astype(jnp.int32)).astype(F32).astype(BF16) for s in range(nc)]
    matches = jnp.concatenate(matches + matches, axis=1)
    nt = (((1,), (1,)), ((), ()))

    def one_block(n, carry):
        def one_source(s, inner):
            values = got_ref[s, 0:ed, :]
            dofs = got_ref[s, ed : 2 * ed, :].astype(jnp.int32) - n * block
            for half in range(block // rows):
                total = jnp.zeros((rows, cap), F32)
                for i in range(ed):
                    hit = base == dofs[i : i + 1, :] - half * rows
                    total = jnp.where(hit, values[i : i + 1, :], total)
                high = total.astype(BF16)
                at = pl.ds(pl.multiple_of(s * cap, cap), cap)
                spread_ref[half * rows : (half + 1) * rows, at] = high
                at = pl.ds(pl.multiple_of((s + nc) * cap, cap), cap)
                spread_ref[half * rows : (half + 1) * rows, at] = (total - high.astype(F32)).astype(BF16)
            return inner

        lax.fori_loop(0, nc, one_source, 0)
        at = pl.ds(pl.multiple_of(n * block, block), block)
        summed = lax.dot_general(matches, spread_ref[...], nt, preferred_element_type=F32)
        rhs_ref[:, at] = summed + slope_ref[...] * mass_ref[:, at]
        return carry

    lax.fori_loop(0, width // block, one_block, 0)


def on_device(nc, nb, diag_inverse, coupling, elem_stiff, elem_mass, elem_dofs, elem_slab, elem_var, mode, mass_mode, eigenvalue):
    band = lax.axis_index("band")
    cols, width = diag_inverse.shape
    ed, count = elem_dofs.shape
    cap = count // 4
    everyone = nc * nb
    vmem = pl.BlockSpec(memory_space=pltpu.VMEM)
    diag_blocks = replicate_chain(diag_inverse, nc)
    coup_blocks = replicate_chain(coupling, nc)
    table = lax.all_to_all(jnp.broadcast_to(mode[None, :], (everyone, cols)), ("chain", "band"), 0, 0, tiled=True)
    send, slope = pl.pallas_call(
        functools.partial(loads_kernel, nc, VARS),
        out_shape=(jax.ShapeDtypeStruct((nc, 2 * ed + 8, cap), F32), jax.ShapeDtypeStruct((1, VARS), F32)),
        in_specs=[pl.BlockSpec(memory_space=pltpu.SMEM)] + [vmem] * 6,
        out_specs=(vmem, vmem),
        scratch_shapes=[pltpu.VMEM((ed, count), F32), pltpu.VMEM((ed, count), F32)],
        compiler_params=pltpu.CompilerParams(vmem_limit_bytes=30 * 1024 * 1024),
        cost_estimate=pl.CostEstimate(flops=2 * 10**9, bytes_accessed=10**7, transcendentals=0),
        name="loads",
    )(eigenvalue, table, elem_stiff, elem_mass, elem_dofs, elem_slab.reshape(1, count), elem_var.reshape(1, count))
    got = lax.all_to_all(send, "chain", 0, 0, tiled=True)
    slopes = lax.all_to_all(jnp.broadcast_to(slope, (everyone, VARS)), ("chain", "band"), 0, 0, tiled=True)
    eigval_slope = jnp.sum(slopes, axis=0)
    own = lax.broadcasted_iota(jnp.int32, (1, width), 1) // cols == band
    own_mass = jnp.where(own, mass_mode[None, :], 0.0)
    rhs = pl.pallas_call(
        functools.partial(scatter_kernel, nc),
        out_shape=jax.ShapeDtypeStruct((VARS, width), F32),
        in_specs=[vmem] * 3,
        out_specs=vmem,
        scratch_shapes=[pltpu.VMEM((256, 2 * nc * cap), BF16)],
        compiler_params=pltpu.CompilerParams(vmem_limit_bytes=30 * 1024 * 1024),
        cost_estimate=pl.CostEstimate(flops=5 * 10**9, bytes_accessed=10**7, transcendentals=0),
        name="scatter",
    )(got, eigval_slope[:, None], own_mass)
    rhs = lax.all_to_all(rhs.reshape(nc, VARS // nc, width), "chain", 0, 0, tiled=True)
    return sweep(diag_blocks, coup_blocks, rhs, nc, nb), eigval_slope


def solution(mesh):
    nc, nb = mesh.shape["chain"], mesh.shape["band"]
    in_specs = (
        P(("chain", "band"), None),
        P("chain", "band"),
        P(None, None, ("chain", "band")),
        P(None, None, ("chain", "band")),
        P(None, ("chain", "band")),
        P(("chain", "band"), None),
        P(("chain", "band")),
        P(("chain", "band")),
        P("chain"),
        P(),
    )
    out_specs = (P(None, ("chain", "band")), P())
    return jax.shard_map(functools.partial(on_device, nc, nb), mesh=mesh, in_specs=in_specs, out_specs=out_specs, check_vma=False)
```

time: 2480 us -> 377 us (0.15)
  waiting for transfers between devices: 1940 us -> 104 us
  Pallas kernels: 0 us -> 228 us
  other arithmetic: 145 us -> 0.16 us
  local copies, waits for them, and re-layouts: 123 us -> 7.5 us
  blocking collectives: 112 us -> 0 us
  matrix products: 92.1 us -> 0 us
    psum x22 -> x0, waiting for transfers between devices: 1900 us -> none  [advance(): summed = lax.psum(partial_value, 'band')]
    pallas_call x0 -> x3, Pallas kernels: none -> 228 us  [the longest x1 194 us: sweep(): pl.pallas_call(functools.partial(sweep_kernel, nc, nb), out_shape=jax.Sha...]
    scatter-add x1 -> x0, other arithmetic: 130 us -> none  [on_device(): assembled = jnp.zeros((VARS * slab_rows,), jnp.float32).at[got_index.resh...]
    all_to_all x2 -> x4, waiting for transfers between devices: 5.61 us -> 104 us  [the longest x1 59.7 us: on_device(): lax.all_to_all(jnp.broadcast_to(mode[None, :], (everyone, cols)), ('chain...]
    dot_general x45 -> x0, matrix products: 92.1 us -> none  [the longest x11 32.3 us: forward_prepare(): lax.dot_general(received, coupling, contract, precision=highest, preferre...]
    gather x2 -> x0, local copies, waits for them, and re-layouts: 68 us -> none  [on_device(): mode_at = whole_mode[dof_index]]
    psum x1 -> x0, blocking collectives: 64.9 us -> none  [on_device(): eigval_slope = lax.psum(local_slope, ('chain', 'band'))]
    scatter x4 -> x0, local copies, waits for them, and re-layouts: 50.9 us -> none  [the longest x2 25.5 us: on_device(): send_index = jnp.zeros((chain_len, elem_width, capacity), jnp.int32).at[d...]
  transfers between devices with their start and end apart: 46 -> 18, of which waited for: 45 -> 4; matrix products, arithmetic and copies ran while one was open for 4% -> 1% of each run, Pallas kernels for 0% -> 9%
where the time goes in v1:
time: 377 us
  Pallas kernels  228 us (60%)
  waiting for transfers between devices  104 us (28%)
  starting transfers between devices  35.3 us (9%)
  local copies, waits for them, and re-layouts  7.5 us (2%)
    pallas_call x1, Pallas kernels, sweep(): pl.pallas_call(functools.partial(sweep_kernel, nc, nb), out_shape=jax.Sha...  194 us
    all_to_all x1, waiting for transfers between devices, on_device(): lax.all_to_all(jnp.broadcast_to(mode[None, :], (everyone, cols)), ('chain...  59.7 us
    pallas_call x1, Pallas kernels, on_device(): pl.pallas_call(functools.partial(scatter_kernel, nc), out_shape=jax.Shape...  27 us
    all_to_all x1, waiting for transfers between devices, on_device(): lax.all_to_all(rhs.reshape(nc, VARS // nc, width), 'chain', 0, 0, tiled=T...  20.2 us
    all_to_all x1, waiting for transfers between devices, on_device(): got = lax.all_to_all(send, 'chain', 0, 0, tiled=True)  17.8 us
    all_to_all x1, starting transfers between devices, on_device(): lax.all_to_all(jnp.broadcast_to(mode[None, :], (everyone, cols)), ('chain...  10.9 us
    ppermute x6, starting transfers between devices, replicate_chain(): moved = lax.ppermute(block, 'chain', pairs)  8.09 us
  transfers between devices with their start and end apart: 18, of which 4 were waited for; matrix products, arithmetic and copies ran while one was open for 1% of the time, Pallas kernels for 9%

profile of v1, /device:TPU:0, one launch (start us, length us, event | category | flops | bytes accessed | tf_op | source)
XLA Modules:
  0.0 376.8 jit_solution(10300950585401931099)
XLA Ops:
  0.6 3.2 collective-permute-start.10
  3.8 1.1 collective-permute-start.12
  5.0 0.9 collective-permute-start.1
  5.8 0.6 collective-permute-start.3
  6.5 1.3 broadcast_in_dim.10
  7.8 10.9 %all-to-all-start = ((f32[128,1,128]{2,1,0:T(1,128)}), f32[128,1,128]{2,1,0:T(1,128)S(1)}, u32[]{:S(2)}, u32[]{:S(2)}) async-start(f32[128,1,128]{2,1,0:T(1,128)} %broadcast_in_dim.10), calls=%async_computation | async-start | bytes 131072 | tf_op jit(solution)/shard_map/all_to_all | solution.py:333
  19.4 59.7 %all-to-all-done = f32[128,1,128]{2,1,0:T(1,128)S(1)} async-done(((f32[128,1,128]{2,1,0:T(1,128)}), f32[128,1,128]{2,1,0:T(1,128)S(1)}, u32[]{:S(2)}, u32[]{:S(2)}) %all-to-all-start) | async-done | bytes 65568 | tf_op jit(solution)/shard_map/all_to_all | solution.py:333
  79.1 0.0 copy-start.1
  79.1 1.3 copy-done.1
  80.4 0.0 copy-start.2
  80.4 1.3 copy-done.2
  81.6 0.0 copy-start.3
  81.6 0.8 copy-done.3
  82.4 0.0 copy-start.4
  82.4 0.7 copy-done.4
  83.1 0.0 copy-start.5
  83.1 0.7 copy-done.5
  83.8 0.0 copy-start
  83.8 0.0 copy-start.6
  83.8 7.0 %loads.1 = (f32[8,56,128]{2,1,0:T(8,128)}, f32[1,192]{1,0:T(1,128)S(1)}) custom-call(f32[1]{0:T(128)S(6)} %copy.19.lam_ref, f32[128,128]{1,0:T(8,128)S(1)} %bitcast.7, f32[24,24,512]{2,1,0:T(8,128)S(1)} %copy-done.1, f32[24,24,512]{2,1,0:T(8,128)S(1)} %copy-done.2, s32[24,512]{1,0:T(8,128)S(1)} %copy-done.3, s32[1,512]{1,0:T(1,128)S(1)} %bitcast.10, ...), custom_call_target="tpu_custom_call" | custom-call | flops 2000000000 | bytes 10000000 | tf_op jit(solution)/shard_map/loads/pallas_call | solution.py:334
  90.8 0.7 broadcast_in_dim.20
  91.5 6.5 %all-to-all-start.2 = ((f32[128,1,192]{2,1,0:T(1,128)}), f32[128,1,192]{2,1,0:T(1,128)S(1)}, u32[]{:S(2)}, u32[]{:S(2)}) async-start(f32[128,1,192]{2,1,0:T(1,128)} %broadcast_in_dim.20), calls=%async_computation.2 | async-start | bytes 262144 | tf_op jit(solution)/shard_map/all_to_all | solution.py:345
  98.0 0.0 copy-done
  98.0 2.2 collective-permute-start.5
  100.3 0.0 collective-permute-done.10.refs_12_
  100.3 0.0 collective-permute-start.8
  100.3 0.0 collective-permute-done.12.refs_14_
  100.3 0.1 collective-permute-start
  100.4 0.0 collective-permute-done.1.refs_2_
  100.4 0.5 collective-permute-start.7
  100.9 0.0 collective-permute-done.3.refs_4_
  100.9 0.1 collective-permute-start.11
  101.0 6.6 %all-to-all-done.2 = f32[128,1,192]{2,1,0:T(1,128)S(1)} async-done(((f32[128,1,192]{2,1,0:T(1,128)}), f32[128,1,192]{2,1,0:T(1,128)S(1)}, u32[]{:S(2)}, u32[]{:S(2)}) %all-to-all-start.2) | async-done | bytes 98336 | tf_op jit(solution)/shard_map/all_to_all | solution.py:345
  107.6 3.4 all-to-all-start.1
  111.0 0.0 copy-done.6
  111.0 0.2 reduce_sum.9
  111.2 0.0 copy-start.7
  111.2 0.1 copy.16.slope_ref
  111.3 17.8 %all-to-all-done.1.got_ref = f32[8,56,128]{2,1,0:T(8,128)S(1)} async-done(((f32[8,56,128]{2,1,0:T(8,128)}), f32[8,56,128]{2,1,0:T(8,128)S(1)}, u32[]{:S(2)}, u32[]{:S(2)}) %all-to-all-start.1) | async-done | bytes 229408 | tf_op jit(solution)/shard_map/all_to_all | solution.py:344
  129.1 27.0 %scatter.1 = f32[192,2048]{1,0:T(8,128)} custom-call(f32[8,56,128]{2,1,0:T(8,128)S(1)} %all-to-all-done.1.got_ref, f32[192,1]{1,0:T(8,128)S(1)} %copy.16.slope_ref, f32[1,2048]{1,0:T(1,128)S(1)} %bitcast.8), custom_call_target="tpu_custom_call" | custom-call | flops 5000000000 | bytes 10000000 | tf_op jit(solution)/shard_map/scatter/pallas_call | solution.py:349
  156.1 0.0 copy-done.7
  156.1 4.3 %all-to-all-start.3 = ((f32[8,24,2048]{2,1,0:T(8,128)}), f32[8,24,2048]{2,1,0:T(8,128)}, u32[]{:S(2)}, u32[]{:S(2)}) async-start(f32[8,24,2048]{2,1,0:T(8,128)} %bitcast.6), calls=%async_computation.3 | async-start | bytes 3145728 | tf_op jit(solution)/shard_map/all_to_all | solution.py:359
  160.4 0.0 collective-permute-done.5.refs_6_
  160.4 0.4 collective-permute-start.13
  160.8 0.0 collective-permute-done.8.refs_10_
  160.8 0.2 collective-permute-start.2
  161.0 0.0 collective-permute-done.refs_1_
  161.0 0.3 collective-permute-start.4
  161.3 0.0 collective-permute-done.7.refs_9_
  161.3 0.2 collective-permute-start.6
  161.5 0.0 collective-permute-done.11.refs_13_
  161.5 0.3 collective-permute-start.9
  161.8 20.2 %all-to-all-done.3.refs_16_ = f32[8,24,2048]{2,1,0:T(8,128)} async-done(((f32[8,24,2048]{2,1,0:T(8,128)}), f32[8,24,2048]{2,1,0:T(8,128)}, u32[]{:S(2)}, u32[]{:S(2)}) %all-to-all-start.3) | async-done | bytes 1572896 | tf_op jit(solution)/shard_map/all_to_all | solution.py:359
  182.0 0.0 collective-permute-done.13.refs_15_
  182.0 0.0 collective-permute-done.2.refs_3_
  182.0 0.0 collective-permute-done.4.refs_5_
  182.0 0.0 collective-permute-done.6.refs_7_
  182.0 0.0 collective-permute-done.9.refs_11_
  182.0 194.1 %sweep.1 = f32[192,128]{1,0:T(8,128)S(1)} custom-call(f32[128,2048]{1,0:T(8,128)S(1)} %copy-done, f32[128,2048]{1,0:T(8,128)S(1)} %collective-permute-done.refs_1_, f32[128,2048]{1,0:T(8,128)S(1)} %collective-permute-done.1.refs_2_, f32[128,2048]{1,0:T(8,128)} %collective-permute-done.2.refs_3_, f32[128,2048]{1,0:T(8,128)} %collective-permute-done.3.refs_4_, ...), custom_call_target="tpu_custom_call" | custom-call | flops 1610612736 | bytes 16777216 | tf_op jit(solution)/shard_map/sweep/pallas_call | solution.py:178
  376.1 0.6 copy.20
  (1 shorter events, 0.0 us)
Async XLA Ops:
  0.6 99.6 %collective-permute-start.10 = (f32[2048,128]{1,0:T(8,128)}, f32[2048,128]{1,0:T(8,128)}, u32[]{:S(2)}, u32[]{:S(2)}) collective-permute-start(f32[2048,128]{1,0:T(8,128)} %refs_8_.1), channel_id=1, source_target_pairs={{0,64},{16,80},{32,96},{48,112},{64,0},{80,16},{96,32},{112,48},{1... | collective-permute-start | bytes 3145736 | tf_op jit(solution)/shard_map/ppermute | solution.py:215
  3.8 96.4 %collective-permute-start.12 = (f32[2048,128]{1,0:T(8,128)}, f32[2048,128]{1,0:T(8,128)}, u32[]{:S(2)}, u32[]{:S(2)}) collective-permute-start(f32[2048,128]{1,0:T(8,128)} %refs_8_.1), channel_id=1, source_target_pairs={{0,96},{16,112},{32,0},{48,16},{64,32},{80,48},{96,64},{112,80},{1... | collective-permute-start | bytes 3145736 | tf_op jit(solution)/shard_map/ppermute | solution.py:215
  5.0 95.4 %collective-permute-start.1 = (f32[128,2048]{1,0:T(8,128)}, f32[128,2048]{1,0:T(8,128)S(1)}, u32[]{:S(2)}, u32[]{:S(2)}) collective-permute-start(f32[128,2048]{1,0:T(8,128)} %refs_0_.1), channel_id=1, source_target_pairs={{0,32},{16,48},{32,64},{48,80},{64,96},{80,112},{96,0},{112,16},{1... | collective-permute-start | bytes 3145736 | tf_op jit(solution)/shard_map/ppermute | solution.py:215
  5.8 95.0 %collective-permute-start.3 = (f32[128,2048]{1,0:T(8,128)}, f32[128,2048]{1,0:T(8,128)}, u32[]{:S(2)}, u32[]{:S(2)}) collective-permute-start(f32[128,2048]{1,0:T(8,128)} %refs_0_.1), channel_id=1, source_target_pairs={{0,64},{16,80},{32,96},{48,112},{64,0},{80,16},{96,32},{112,48},{1... | collective-permute-start | bytes 3145736 | tf_op jit(solution)/shard_map/ppermute | solution.py:215
  7.8 71.3 %all-to-all-start = ((f32[128,1,128]{2,1,0:T(1,128)}), f32[128,1,128]{2,1,0:T(1,128)S(1)}, u32[]{:S(2)}, u32[]{:S(2)}) async-start(f32[128,1,128]{2,1,0:T(1,128)} %broadcast_in_dim.10), calls=%async_computation | async-start | bytes 131072 | tf_op jit(solution)/shard_map/all_to_all | solution.py:333
  79.1 1.3 copy-start.1
  80.4 1.3 copy-start.2
  81.6 0.8 copy-start.3
  82.4 0.7 copy-start.4
  83.1 0.7 copy-start.5
  83.8 14.2 %copy-start = (f32[128,2048]{1,0:T(8,128)S(1)}, f32[128,2048]{1,0:T(8,128)}, u32[]{:S(2)}) copy-start(f32[128,2048]{1,0:T(8,128)} %refs_0_.1) | copy-start | bytes 3145732
  83.8 27.2 %copy-start.6 = (f32[2048]{0:T(1024)S(1)}, f32[2048]{0:T(1024)}, u32[]{:S(2)}) copy-start(f32[2048]{0:T(1024)} %param.18) | copy-start | bytes 24580
  91.5 16.1 %all-to-all-start.2 = ((f32[128,1,192]{2,1,0:T(1,128)}), f32[128,1,192]{2,1,0:T(1,128)S(1)}, u32[]{:S(2)}, u32[]{:S(2)}) async-start(f32[128,1,192]{2,1,0:T(1,128)} %broadcast_in_dim.20), calls=%async_computation.2 | async-start | bytes 262144 | tf_op jit(solution)/shard_map/all_to_all | solution.py:345
  98.0 62.4 %collective-permute-start.5 = (f32[128,2048]{1,0:T(8,128)S(1)}, f32[128,2048]{1,0:T(8,128)}, u32[]{:S(2)}, u32[]{:S(2)}) collective-permute-start(f32[128,2048]{1,0:T(8,128)S(1)} %copy-done), channel_id=1, source_target_pairs={{0,96},{16,112},{32,0},{48,16},{64,32},{80,48},{96,64},{112,80},{1... | collective-permute-start | bytes 3145736 | tf_op jit(solution)/shard_map/ppermute | solution.py:215
  100.3 60.5 %collective-permute-start.8 = (f32[2048,128]{1,0:T(8,128)}, f32[2048,128]{1,0:T(8,128)}, u32[]{:S(2)}, u32[]{:S(2)}) collective-permute-start(f32[2048,128]{1,0:T(8,128)} %refs_8_.1), channel_id=1, source_target_pairs={{0,32},{16,48},{32,64},{48,80},{64,96},{80,112},{96,0},{112,16},{1... | collective-permute-start | bytes 3145736 | tf_op jit(solution)/shard_map/ppermute | solution.py:215
  100.3 60.7 %collective-permute-start = (f32[128,2048]{1,0:T(8,128)S(1)}, f32[128,2048]{1,0:T(8,128)S(1)}, u32[]{:S(2)}, u32[]{:S(2)}) collective-permute-start(f32[128,2048]{1,0:T(8,128)S(1)} %copy-done), channel_id=1, source_target_pairs={{0,16},{16,0},{32,48},{48,32},{64,80},{80,64},{96,112},{112,96},{1... | collective-permute-start | bytes 3145736 | tf_op jit(solution)/shard_map/ppermute | solution.py:220
  100.4 60.9 %collective-permute-start.7 = (f32[2048,128]{1,0:T(8,128)}, f32[2048,128]{1,0:T(8,128)}, u32[]{:S(2)}, u32[]{:S(2)}) collective-permute-start(f32[2048,128]{1,0:T(8,128)} %refs_8_.1), channel_id=1, source_target_pairs={{0,16},{16,0},{32,48},{48,32},{64,80},{80,64},{96,112},{112,96},{1... | collective-permute-start | bytes 3145736 | tf_op jit(solution)/shard_map/ppermute | solution.py:220
  100.9 60.6 %collective-permute-start.11 = (f32[2048,128]{1,0:T(8,128)}, f32[2048,128]{1,0:T(8,128)}, u32[]{:S(2)}, u32[]{:S(2)}) collective-permute-start(f32[2048,128]{1,0:T(8,128)} %collective-permute-done.10.refs_12_), channel_id=1, source_target_pairs={{0,16},{16,0},{32,48},{48,32},{64,80},{80,64},{96,112},{112,96},{1... | collective-permute-start | bytes 3145736 | tf_op jit(solution)/shard_map/ppermute | solution.py:220
  107.6 21.5 %all-to-all-start.1 = ((f32[8,56,128]{2,1,0:T(8,128)}), f32[8,56,128]{2,1,0:T(8,128)S(1)}, u32[]{:S(2)}, u32[]{:S(2)}) async-start(f32[8,56,128]{2,1,0:T(8,128)} %get-tuple-element.4), calls=%async_computation.1 | async-start | bytes 458752 | tf_op jit(solution)/shard_map/all_to_all | solution.py:344
  111.2 44.9 %copy-start.7 = (f32[192]{0:T(256)}, f32[192]{0:T(256)S(1)}, u32[]{:S(2)}) copy-start(f32[192]{0:T(256)S(1)} %reduce_sum.9) | copy-start | bytes 2308
  156.1 25.9 %all-to-all-start.3 = ((f32[8,24,2048]{2,1,0:T(8,128)}), f32[8,24,2048]{2,1,0:T(8,128)}, u32[]{:S(2)}, u32[]{:S(2)}) async-start(f32[8,24,2048]{2,1,0:T(8,128)} %bitcast.6), calls=%async_computation.3 | async-start | bytes 3145728 | tf_op jit(solution)/shard_map/all_to_all | solution.py:359
  160.4 21.6 %collective-permute-start.13 = (f32[2048,128]{1,0:T(8,128)}, f32[2048,128]{1,0:T(8,128)}, u32[]{:S(2)}, u32[]{:S(2)}) collective-permute-start(f32[2048,128]{1,0:T(8,128)} %collective-permute-done.12.refs_14_), channel_id=1, source_target_pairs={{0,16},{16,0},{32,48},{48,32},{64,80},{80,64},{96,112},{112,96},{1... | collective-permute-start | bytes 3145736 | tf_op jit(solution)/shard_map/ppermute | solution.py:220
  160.8 21.2 %collective-permute-start.2 = (f32[128,2048]{1,0:T(8,128)S(1)}, f32[128,2048]{1,0:T(8,128)}, u32[]{:S(2)}, u32[]{:S(2)}) collective-permute-start(f32[128,2048]{1,0:T(8,128)S(1)} %collective-permute-done.1.refs_2_), channel_id=1, source_target_pairs={{0,16},{16,0},{32,48},{48,32},{64,80},{80,64},{96,112},{112,96},{1... | collective-permute-start | bytes 3145736 | tf_op jit(solution)/shard_map/ppermute | solution.py:220
  161.0 21.0 %collective-permute-start.4 = (f32[128,2048]{1,0:T(8,128)}, f32[128,2048]{1,0:T(8,128)}, u32[]{:S(2)}, u32[]{:S(2)}) collective-permute-start(f32[128,2048]{1,0:T(8,128)} %collective-permute-done.3.refs_4_), channel_id=1, source_target_pairs={{0,16},{16,0},{32,48},{48,32},{64,80},{80,64},{96,112},{112,96},{1... | collective-permute-start | bytes 3145736 | tf_op jit(solution)/shard_map/ppermute | solution.py:220
  161.3 20.7 %collective-permute-start.6 = (f32[128,2048]{1,0:T(8,128)}, f32[128,2048]{1,0:T(8,128)}, u32[]{:S(2)}, u32[]{:S(2)}) collective-permute-start(f32[128,2048]{1,0:T(8,128)} %collective-permute-done.5.refs_6_), channel_id=1, source_target_pairs={{0,16},{16,0},{32,48},{48,32},{64,80},{80,64},{96,112},{112,96},{1... | collective-permute-start | bytes 3145736 | tf_op jit(solution)/shard_map/ppermute | solution.py:220
  161.5 20.5 %collective-permute-start.9 = (f32[2048,128]{1,0:T(8,128)}, f32[2048,128]{1,0:T(8,128)}, u32[]{:S(2)}, u32[]{:S(2)}) collective-permute-start(f32[2048,128]{1,0:T(8,128)} %collective-permute-done.8.refs_10_), channel_id=1, source_target_pairs={{0,16},{16,0},{32,48},{48,32},{64,80},{80,64},{96,112},{112,96},{1... | collective-permute-start | bytes 3145736 | tf_op jit(solution)/shard_map/ppermute | solution.py:220

commit v2 on v1

v2 whole, which is shorter than its diff:
```python
import functools

import jax
import jax.numpy as jnp
from jax import lax
from jax.experimental import pallas as pl
from jax.experimental.pallas import tpu as pltpu
from jax.sharding import PartitionSpec as P

MESH = pl.DeviceIdType.MESH
F32 = jnp.float32
BF16 = jnp.bfloat16
VARS = 192


def split2(x):
    high = x.astype(BF16)
    return high, (x - high.astype(F32)).astype(BF16)


def stacked_rows(x):
    high = x.astype(BF16).astype(F32)
    return jnp.concatenate([high, x - high], axis=0).astype(BF16)


def three_way(x):
    high = x.astype(BF16).astype(F32)
    middle = (x - high).astype(BF16).astype(F32)
    return high, middle, x - high - middle


def loads_kernel(nc, lam_ref, table_ref, stiff_ref, mass_ref, dofs_ref, slab_ref, var_ref,
                 send_ref, slope_ref, mode_at, loads):
    ed, count = dofs_ref.shape
    lanes = table_ref.shape[1]
    cap = send_ref.shape[2]
    per_slab = table_ref.shape[0] // nc
    lam = lam_ref[0]
    dofs, slab, var = dofs_ref[...], slab_ref[...], var_ref[...]
    row_of = slab * per_slab + lax.shift_right_logical(dofs, 7)
    lane_of = jnp.bitwise_and(dofs, lanes - 1)
    chunks = count // lanes

    def look(step, found):
        found = list(found)
        for inner in range(8):
            r = step * 8 + inner
            row = jnp.broadcast_to(table_ref[pl.ds(r, 1), :], (ed, lanes))
            for c in range(chunks):
                at = slice(c * lanes, (c + 1) * lanes)
                taken = jnp.take_along_axis(row, lane_of[:, at], axis=1, mode="promise_in_bounds")
                found[c] = jnp.where(row_of[:, at] == r, taken, found[c])
        return tuple(found)

    found = lax.fori_loop(0, table_ref.shape[0] // 8, look, (jnp.zeros((ed, lanes), F32),) * chunks)
    for c in range(chunks):
        mode_at[:, c * lanes : (c + 1) * lanes] = found[c]
    modes = mode_at[...]
    for i in range(ed):
        operator = stiff_ref[i] - lam * mass_ref[i]
        loads[i : i + 1, :] = -jnp.sum(operator * modes, axis=0, keepdims=True)
    values = loads[...]
    quadratic = -jnp.sum(modes * values, axis=0, keepdims=True)
    padded = slope_ref.shape[1]
    matches = (lax.broadcasted_iota(jnp.int32, (padded, count), 0) == var).astype(F32).astype(BF16)
    terms = jnp.concatenate(list(three_way(quadratic)) + [jnp.zeros((5, count), F32)], axis=0).astype(BF16)
    nt = (((1,), (1,)), ((), ()))
    sums = lax.dot_general(terms, matches, nt, preferred_element_type=F32)
    slope_ref[...] = jnp.broadcast_to(jnp.sum(sums, axis=0, keepdims=True), slope_ref.shape)
    merged = jnp.zeros((ed, count), F32)
    for i in range(ed):
        merged = merged + jnp.where(dofs == dofs[i : i + 1, :], values[i : i + 1, :], 0.0)
    onehot = (lax.broadcasted_iota(jnp.int32, (nc, count), 0) == slab).astype(F32)
    earlier = lax.broadcasted_iota(jnp.int32, (count, count), 0) < lax.broadcasted_iota(jnp.int32, (count, count), 1)
    rank_all = jnp.dot(onehot.astype(BF16), earlier.astype(F32).astype(BF16), preferred_element_type=F32)
    rank = jnp.sum(onehot * rank_all, axis=0, keepdims=True).astype(jnp.int32)
    slot = slab * cap + rank
    high, middle, low = three_way(merged)
    coarse = lax.shift_right_logical(dofs, 4).astype(F32)
    fine = jnp.bitwise_and(dofs, 15).astype(F32)
    var_rows = jnp.concatenate([var.astype(F32), jnp.zeros((7, count), F32)], axis=0)
    data = jnp.concatenate([high, middle, low, coarse, fine, var_rows], axis=0).astype(BF16)
    for k in range(nc):
        place = (lax.broadcasted_iota(jnp.int32, (cap, count), 0) + k * cap == slot).astype(F32).astype(BF16)
        packed = lax.dot_general(data, place, nt, preferred_element_type=F32)
        send_ref[k, 0:ed, :] = (packed[0:ed] + packed[ed : 2 * ed]) + packed[2 * ed : 3 * ed]
        send_ref[k, ed : 2 * ed, :] = packed[3 * ed : 4 * ed] * 16.0 + packed[4 * ed : 5 * ed]
        send_ref[k, 2 * ed : 2 * ed + 8, :] = packed[5 * ed : 5 * ed + 8]


def solve_kernel(nc, nb, diag_ref, coup_ref, got_ref, slope_ref, mass_ref, out_ref, slope_out,
                 dbuf, cbuf, dsplit, csplit, spread_ref, rpart, rbuf, sl_chain, sl_band,
                 part, slots, piece, full, ybuf, xbuf,
                 mat, own_send, relay_send, slc_send, slc_recv, slb_send, slb_recv, r_send, r_recv,
                 rs_send, rs_recv, ag_send, ag_recv, out_send, out_recv):
    me, band = lax.axis_index("chain"), lax.axis_index("band")
    x_len = nc // 2
    my_x, core = me // 2, lax.rem(me, 2)
    rows, width = part.shape
    cols = width // nb
    nvars = rpart.shape[0]
    sibling = 2 * my_x + 1 - core
    blocks = (dbuf, cbuf)
    nt = (((1,), (1,)), ((), ()))
    nn = (((1,), (0,)), ((), ()))

    def at_band(b):
        return pl.ds(pl.multiple_of(b * cols, cols), cols)

    def at_group(c):
        return pl.ds(pl.multiple_of(c * rows, 8), rows)

    def along_x(by):
        return 2 * lax.rem(my_x + by + x_len, x_len) + core

    def remote(src, dst, send, recv, chain, to_band):
        return pltpu.make_async_remote_copy(src_ref=src, dst_ref=dst, send_sem=send, recv_sem=recv,
                                            device_id=(chain, to_band), device_id_type=MESH)

    def each_block(which, work):
        if which == 0:
            work()
        else:
            pl.when(me != 0)(work)

    def own_load(which):
        return pltpu.make_async_copy((diag_ref, coup_ref)[which], blocks[which].at[me], mat.at[which, me])

    def own_copy(which, i):
        to = (along_x(1), along_x(-1), sibling)[i]
        return remote((diag_ref, coup_ref)[which], blocks[which].at[me], own_send.at[which, i], mat.at[which, me], to, band)

    for which in range(2):
        each_block(which, lambda which=which: own_load(which).start())

    barrier = pltpu.get_barrier_semaphore()
    for r in range(1, nb):
        pl.semaphore_signal(barrier, inc=1, device_id=(me, lax.rem(band + r, nb)), device_id_type=MESH)
    for r in range(1, nc):
        pl.semaphore_signal(barrier, inc=1, device_id=(lax.rem(me + r, nc), band), device_id_type=MESH)
    pl.semaphore_wait(barrier, nb + nc - 2)

    def slope_chain_copy(to, source):
        return remote(slope_ref, sl_chain.at[source], slc_send.at[to], slc_recv.at[source], to, band)

    for r in range(1, nc):
        slope_chain_copy(lax.rem(me + r, nc), me).start()
    sl_chain[me] = slope_ref[...]

    def send_own(which):
        for i in range(3):
            own_copy(which, i).start()

    for which in range(2):
        each_block(which, functools.partial(send_own, which))

    def relay_copies(which, by):
        slab = along_x(-by)
        block = blocks[which].at[slab]
        on = remote(block, block, relay_send.at[which, by, 0], mat.at[which, slab], sibling, band)
        further = remote(block, block, relay_send.at[which, by, 1], mat.at[which, slab], along_x(1 if by == 1 else -1), band)
        return slab, on, further

    def forwards(by):
        return {1: core == 0, 3: core == 1}[by]

    def relay(which, by):
        slab, on, further = relay_copies(which, by)

        def work():
            pltpu.make_async_copy(blocks[which].at[slab], blocks[which].at[slab], mat.at[which, slab]).wait()
            on.start()
            if by != 2:
                pl.when(forwards(by))(lambda: further.start())

        if which == 0:
            work()
        else:
            pl.when(slab != 0)(work)

    def relay_farthest(which, k):
        pl.when(k == along_x(2))(lambda: relay(which, 2))

    cap = got_ref.shape[2]
    ed = (got_ref.shape[1] - 8) // 2
    block = spread_ref.shape[0]
    lines = 128
    base = lax.broadcasted_iota(jnp.int32, (lines, cap), 0)
    variable = lax.broadcasted_iota(jnp.int32, (nvars, cap), 0)
    matches = [(variable == got_ref[s, 2 * ed : 2 * ed + 1, :].astype(jnp.int32)).astype(F32).astype(BF16) for s in range(nc)]
    matches = jnp.concatenate(matches + matches, axis=1)

    def one_block(n, carry):
        def one_source(s, inner):
            values = got_ref[s, 0:ed, :]
            dofs = got_ref[s, ed : 2 * ed, :].astype(jnp.int32) - n * block
            for half in range(block // lines):
                total = jnp.zeros((lines, cap), F32)
                for i in range(ed):
                    hit = base == dofs[i : i + 1, :] - half * lines
                    total = jnp.where(hit, values[i : i + 1, :], total)
                high = total.astype(BF16)
                at = pl.ds(pl.multiple_of(s * cap, cap), cap)
                spread_ref[half * lines : (half + 1) * lines, at] = high
                at = pl.ds(pl.multiple_of((s + nc) * cap, cap), cap)
                spread_ref[half * lines : (half + 1) * lines, at] = (total - high.astype(F32)).astype(BF16)
            return inner

        lax.fori_loop(0, nc, one_source, 0)
        at = pl.ds(pl.multiple_of(n * block, block), block)
        rpart[:, at] = lax.dot_general(matches, spread_ref[...], nt, preferred_element_type=F32)
        return carry

    lax.fori_loop(0, width // block, one_block, 0)

    for r in range(1, nc):
        slope_chain_copy(me, lax.rem(me + r, nc)).wait_recv()
    total = sl_chain[0]
    for c in range(1, nc):
        total = total + sl_chain[c]

    def slope_band_copy(r):
        to = lax.rem(band + r, nb)
        return remote(sl_band.at[band], sl_band.at[band], slb_send.at[r], slb_recv.at[r], me, to)

    def slope_band_arrival(r):
        source = lax.rem(band - r + nb, nb)
        return remote(sl_band.at[source], sl_band.at[source], slb_send.at[r], slb_recv.at[r], me, source)

    sl_band[band] = total
    for r in range(1, nb):
        slope_band_copy(r).start()
    for by in (1, 3):
        relay(0, by)
    for r in range(1, nb):
        slope_band_arrival(r).wait_recv()
    total = sl_band[0]
    for b in range(1, nb):
        total = total + sl_band[b]
    slope_out[...] = total[0:1, :nvars]
    line = lax.broadcasted_iota(jnp.int32, total.shape, 0)
    high, middle, low = three_way(total)
    slope_terms = jnp.where((line == 0) | (line == 3) | (line == 5), high, 0.0)
    slope_terms = jnp.where((line == 1) | (line == 4), middle, jnp.where(line == 2, low, slope_terms))
    line = lax.broadcasted_iota(jnp.int32, (8, cols), 0)
    high, middle, low = three_way(jnp.broadcast_to(mass_ref[...], (8, cols)))
    mass_terms = jnp.where(line < 3, high, jnp.where(line < 5, middle, jnp.where(line == 5, low, 0.0)))
    outer = lax.dot_general(slope_terms.astype(BF16), mass_terms.astype(BF16), (((0,), (0,)), ((), ())), preferred_element_type=F32)
    rpart[:, at_band(band)] = rpart[:, at_band(band)] + outer[:nvars]

    def rhs_copy(to, source):
        return remote(rpart.at[at_group(to), :], rbuf.at[source], r_send.at[to], r_recv.at[source], to, band)

    for r in range(1, nc):
        rhs_copy(lax.rem(me + r, nc), me).start()
    rbuf[me] = rpart[at_group(me), :]
    for by in (1, 3):
        relay(1, by)

    def rhs_wait(k):
        pl.when(k != me)(lambda: rhs_copy(me, k).wait_recv())

    def rs_copy(r):
        to = lax.rem(band + r, nb)
        return remote(part.at[:, at_band(to)], slots.at[r], rs_send.at[r], rs_recv.at[r], me, to)

    def ag_copy(r):
        to = lax.rem(band + r, nb)
        return remote(piece, full.at[:, at_band(band)], ag_send.at[r], ag_recv.at[r], me, to)

    def ag_arrival(r):
        source = lax.rem(band - r + nb, nb)
        return remote(piece, full.at[:, at_band(source)], ag_send.at[r], ag_recv.at[r], me, source)

    def reduce_start():
        for r in range(1, nb):
            rs_copy(r).start()

    def reduce_end():
        total = part[:, at_band(band)]
        for r in range(1, nb):
            rs_copy(r).wait_recv()
            total = total + slots[r]
        for r in range(1, nb):
            rs_copy(r).wait_send()
        return total

    def gather_start(value):
        piece[...] = value
        for r in range(1, nb):
            ag_copy(r).start()
        full[:, at_band(band)] = value

    def gather_end():
        for r in range(1, nb):
            ag_arrival(r).wait_recv()
        for r in range(1, nb):
            ag_copy(r).wait_send()

    def block_wait(which, k):
        @pl.when((lax.rem(k, 2) != core) | (k == me))
        def _():
            pltpu.make_async_copy(blocks[which].at[k], blocks[which].at[k], mat.at[which, k]).wait()

    def split_diag(k):
        block_wait(0, k)
        high, low = split2(dbuf[k])
        dsplit[k, 0:cols, :] = high
        dsplit[k, cols : 2 * cols, :] = low

    def split_coup(k):
        block_wait(1, k)
        high, low = split2(cbuf[k])
        csplit[k, :, 0:cols] = high
        csplit[k, :, cols : 2 * cols] = low

    def narrow(value, weights, dims):
        wide = lax.dot_general(stacked_rows(value), weights, dims, preferred_element_type=F32)
        return (wide[:rows, :cols] + wide[:rows, cols:]) + (wide[rows:, :cols] + wide[rows:, cols:])

    def spread(value, weights, dims):
        both = stacked_rows(value)
        both = jnp.concatenate([both, both], axis=1)
        wide = lax.dot_general(both, weights, dims, preferred_element_type=F32)
        return wide[:rows] + wide[rows:]

    rhs_wait(0)
    part[...] = rbuf[0]
    relay_farthest(0, 0)

    def forward(k, carry):
        reduce_start()
        relay_farthest(0, k + 1)
        relay_farthest(1, k + 1)
        split_diag(k)
        gather_start(reduce_end())

        @pl.when(k + 1 < nc)
        def _():
            split_coup(k + 1)

        gather_end()
        solved = narrow(full[...], dsplit[k], nt)
        ybuf[k] = solved

        @pl.when(k + 1 < nc)
        def _():
            rhs_wait(k + 1)
            part[...] = rbuf[k + 1] - spread(solved, csplit[k + 1], nt)

        return carry

    lax.fori_loop(0, nc, forward, 0)

    def out_copy(k, source):
        return remote(xbuf.at[k], out_ref.at[at_group(source), :], out_send.at[k], out_recv.at[source], k, band)

    def backward(step, coupled):
        k = nc - 1 - step
        part[...] = spread(ybuf[k] - coupled, dsplit[k], nn)
        reduce_start()
        total = reduce_end()
        gather_start(total)
        xbuf[k] = total

        @pl.when(k != me)
        def _():
            out_copy(k, me).start()

        @pl.when(k == me)
        def _():
            out_ref[at_group(me), :] = total

        gather_end()
        return narrow(full[...], csplit[k], nn)

    coupled = lax.fori_loop(0, nc - 1, backward, jnp.zeros((rows, cols), F32))
    part[...] = spread(ybuf[0] - coupled, dsplit[0], nn)
    reduce_start()
    total = reduce_end()
    xbuf[0] = total
    pl.when(me != 0)(lambda: out_copy(0, me).start())

    @pl.when(me == 0)
    def _():
        out_ref[at_group(0), :] = total

    for r in range(1, nc):
        other = lax.rem(me + r, nc)
        out_copy(other, me).wait_send()
        out_copy(me, other).wait_recv()
        rhs_copy(other, me).wait_send()
        slope_chain_copy(other, me).wait_send()
    for r in range(1, nb):
        slope_band_copy(r).wait_send()

    def sent(which):
        for i in range(3):
            own_copy(which, i).wait_send()

    for which in range(2):
        each_block(which, functools.partial(sent, which))
        for by in (1, 2, 3):
            slab, on, further = relay_copies(which, by)

            def relayed(on=on, further=further, by=by):
                on.wait_send()
                if by != 2:
                    pl.when(forwards(by))(lambda: further.wait_send())

            if which == 0:
                relayed()
            else:
                pl.when(slab != 0)(relayed)


def on_device(nc, nb, diag_inverse, coupling, elem_stiff, elem_mass, elem_dofs, elem_slab, elem_var, mode, mass_mode, eigenvalue):
    band = lax.axis_index("band")
    cols, width = diag_inverse.shape
    ed, count = elem_dofs.shape
    cap = count // 4
    rows = VARS // nc
    everyone = nc * nb
    padded = 256
    vmem = pl.BlockSpec(memory_space=pltpu.VMEM)
    anywhere = pl.BlockSpec(memory_space=pl.ANY)
    table = lax.all_to_all(jnp.broadcast_to(mode[None, :], (everyone, cols)), ("chain", "band"), 0, 0, tiled=True)
    send, slope = pl.pallas_call(
        functools.partial(loads_kernel, nc),
        out_shape=(jax.ShapeDtypeStruct((nc, 2 * ed + 8, cap), F32), jax.ShapeDtypeStruct((8, padded), F32)),
        in_specs=[pl.BlockSpec(memory_space=pltpu.SMEM)] + [vmem] * 6,
        out_specs=(vmem, vmem),
        scratch_shapes=[pltpu.VMEM((ed, count), F32), pltpu.VMEM((ed, count), F32)],
        compiler_params=pltpu.CompilerParams(vmem_limit_bytes=30 * 1024 * 1024),
        cost_estimate=pl.CostEstimate(flops=2 * 10**9, bytes_accessed=10**7, transcendentals=0),
        name="loads",
    )(eigenvalue, table, elem_stiff, elem_mass, elem_dofs, elem_slab.reshape(1, count), elem_var.reshape(1, count))
    got = lax.all_to_all(send, "chain", 0, 0, tiled=True)
    own_mass = lax.dynamic_slice_in_dim(mass_mode, band * cols, cols)[None, :]
    dma = pltpu.SemaphoreType.DMA
    eigvec_slope, eigval_slope = pl.pallas_call(
        functools.partial(solve_kernel, nc, nb),
        out_shape=(jax.ShapeDtypeStruct((VARS, cols), F32), jax.ShapeDtypeStruct((1, VARS), F32)),
        in_specs=[anywhere, anywhere, vmem, vmem, vmem],
        out_specs=(vmem, vmem),
        scratch_shapes=[
            pltpu.VMEM((nc, cols, width), F32),
            pltpu.VMEM((nc, width, cols), F32),
            pltpu.VMEM((nc, 2 * cols, width), BF16),
            pltpu.VMEM((nc, width, 2 * cols), BF16),
            pltpu.VMEM((256, 2 * nc * cap), BF16),
            pltpu.VMEM((VARS, width), F32),
            pltpu.VMEM((nc, rows, width), F32),
            pltpu.VMEM((nc, 8, padded), F32),
            pltpu.VMEM((nb, 8, padded), F32),
            pltpu.VMEM((rows, width), F32),
            pltpu.VMEM((nb, rows, cols), F32),
            pltpu.VMEM((rows, cols), F32),
            pltpu.VMEM((rows, width), F32),
            pltpu.VMEM((nc, rows, cols), F32),
            pltpu.VMEM((nc, rows, cols), F32),
            dma((2, nc)), dma((2, 3)), dma((2, 4, 2)),
            dma((nc,)), dma((nc,)), dma((nb,)), dma((nb,)), dma((nc,)), dma((nc,)),
            dma((nb,)), dma((nb,)), dma((nb,)), dma((nb,)), dma((nc,)), dma((nc,)),
        ],
        compiler_params=pltpu.CompilerParams(collective_id=0, has_side_effects=True, vmem_limit_bytes=52 * 1024 * 1024),
        cost_estimate=pl.CostEstimate(flops=10**10, bytes_accessed=10**8, transcendentals=0),
        name="solve",
    )(diag_inverse, coupling, got, slope, own_mass)
    return eigvec_slope, eigval_slope.reshape(VARS)


def solution(mesh):
    nc, nb = mesh.shape["chain"], mesh.shape["band"]
    in_specs = (
        P(("chain", "band"), None),
        P("chain", "band"),
        P(None, None, ("chain", "band")),
        P(None, None, ("chain", "band")),
        P(None, ("chain", "band")),
        P(("chain", "band"), None),
        P(("chain", "band")),
        P(("chain", "band")),
        P("chain"),
        P(),
    )
    out_specs = (P(None, ("chain", "band")), P())
    return jax.shard_map(functools.partial(on_device, nc, nb), mesh=mesh, in_specs=in_specs, out_specs=out_specs, check_vma=False)
```

time: 377 us -> 313 us (0.83)
  waiting for transfers between devices: 104 us -> 15.8 us
  Pallas kernels: 228 us -> 273 us
  starting transfers between devices: 35.3 us -> 14.5 us
    all_to_all x1, waiting for transfers between devices: 59.7 us -> 8.76 us  [on_device(): lax.all_to_all(jnp.broadcast_to(mode[None, :], (everyone, cols)), ('chain...]
    pallas_call x3 -> x2, Pallas kernels: 228 us -> 273 us  [the longest x1 266 us: on_device(): pl.pallas_call(functools.partial(solve_kernel, nc, nb), out_shape=(jax.Sh...]
    all_to_all x2 -> x0, waiting for transfers between devices: 26.8 us -> none  [the longest x1 20.2 us: on_device(): lax.all_to_all(rhs.reshape(nc, VARS // nc, width), 'chain', 0, 0, tiled=T...]
    all_to_all x2 -> x0, starting transfers between devices: 10.8 us -> none  [the longest x1 6.47 us: on_device(): lax.all_to_all(jnp.broadcast_to(slope, (everyone, VARS)), ('chain', 'band...]
    all_to_all x1, waiting for transfers between devices: 17.8 us -> 7.01 us  [on_device(): got = lax.all_to_all(send, 'chain', 0, 0, tiled=True)]
    ppermute x14 -> x0, starting transfers between devices: 10.2 us -> none  [the longest x6 8.09 us: replicate_chain(): moved = lax.ppermute(block, 'chain', pairs)]
  transfers between devices with their start and end apart: 18 -> 2, of which waited for: 4 -> 2; matrix products, arithmetic and copies ran while one was open for 1% -> 0% of each run, Pallas kernels for 9% -> 0%
where the time goes in v2:
time: 313 us; the launch traced here: 312 us
  Pallas kernels  273 us (87%)
  waiting for transfers between devices  15.8 us (5%)
  starting transfers between devices  14.5 us (5%)
  local copies, waits for them, and re-layouts  7.32 us (2%)
    pallas_call x1, Pallas kernels, on_device(): pl.pallas_call(functools.partial(solve_kernel, nc, nb), out_shape=(jax.Sh...  266 us
    all_to_all x1, starting transfers between devices, on_device(): lax.all_to_all(jnp.broadcast_to(mode[None, :], (everyone, cols)), ('chain...  11.1 us
    all_to_all x1, waiting for transfers between devices, on_device(): lax.all_to_all(jnp.broadcast_to(mode[None, :], (everyone, cols)), ('chain...  8.76 us
    pallas_call x1, Pallas kernels, on_device(): pl.pallas_call(functools.partial(loads_kernel, nc), out_shape=(jax.ShapeD...  7.02 us
    all_to_all x1, waiting for transfers between devices, on_device(): got = lax.all_to_all(send, 'chain', 0, 0, tiled=True)  7.01 us
  transfers between devices with their start and end apart: 2, of which 2 were waited for; matrix products, arithmetic and copies ran while one was open for 0% of the time, Pallas kernels for 0%

profile of v2, /device:TPU:0, one launch (start us, length us, event | category | flops | bytes accessed | tf_op | source)
XLA Modules:
  0.0 312.2 jit_solution(13748948238267448538)
XLA Ops:
  0.6 0.0 copy-start
  0.6 1.3 broadcast_in_dim.4
  2.0 11.1 %all-to-all-start = ((f32[128,1,128]{2,1,0:T(1,128)}), f32[128,1,128]{2,1,0:T(1,128)S(1)}, u32[]{:S(2)}, u32[]{:S(2)}) async-start(f32[128,1,128]{2,1,0:T(1,128)} %broadcast_in_dim.4), calls=%async_computation | async-start | bytes 131072 | tf_op jit(solution)/shard_map/all_to_all | solution.py:427
  13.8 8.8 %all-to-all-done = f32[128,1,128]{2,1,0:T(1,128)S(1)} async-done(((f32[128,1,128]{2,1,0:T(1,128)}), f32[128,1,128]{2,1,0:T(1,128)S(1)}, u32[]{:S(2)}, u32[]{:S(2)}) %all-to-all-start) | async-done | bytes 65568 | tf_op jit(solution)/shard_map/all_to_all | solution.py:427
  22.5 0.0 copy-start.1
  22.5 1.3 copy-done.1
  23.8 0.0 copy-start.2
  23.8 1.3 copy-done.2
  25.1 0.0 copy-start.4
  25.1 0.8 copy-done.4
  25.9 0.0 copy-start.5
  25.9 0.7 copy-done.5
  26.6 0.0 copy-start.6
  26.6 0.7 copy-done.6
  27.2 0.0 copy-start.3
  27.2 7.0 %loads.1 = (f32[8,56,128]{2,1,0:T(8,128)}, f32[8,256]{1,0:T(8,128)S(1)}) custom-call(f32[1]{0:T(128)S(6)} %copy.14.lam_ref, f32[128,128]{1,0:T(8,128)S(1)} %bitcast.6, f32[24,24,512]{2,1,0:T(8,128)S(1)} %copy-done.1, f32[24,24,512]{2,1,0:T(8,128)S(1)} %copy-done.2, s32[24,512]{1,0:T(8,128)S(1)} %copy-done.4, s32[1,512]{1,0:T(1,128)S(1)} %bitcast.8, ...), custom_call_target="tpu_custom_call" | custom-call | flops 2000000000 | bytes 10000000 | tf_op jit(solution)/shard_map/loads/pallas_call | solution.py:428
  34.3 3.4 %all-to-all-start.1 = ((f32[8,56,128]{2,1,0:T(8,128)}), f32[8,56,128]{2,1,0:T(8,128)S(1)}, u32[]{:S(2)}, u32[]{:S(2)}) async-start(f32[8,56,128]{2,1,0:T(8,128)} %get-tuple-element.6), calls=%async_computation.1 | async-start | bytes 458752 | tf_op jit(solution)/shard_map/all_to_all | solution.py:438
  37.7 0.0 copy-done
  37.7 0.1 dynamic-slice_bitcast_fusion.mass_ref
  37.8 7.0 %all-to-all-done.1.got_ref = f32[8,56,128]{2,1,0:T(8,128)S(1)} async-done(((f32[8,56,128]{2,1,0:T(8,128)}), f32[8,56,128]{2,1,0:T(8,128)S(1)}, u32[]{:S(2)}, u32[]{:S(2)}) %all-to-all-start.1) | async-done | bytes 229408 | tf_op jit(solution)/shard_map/all_to_all | solution.py:438
  44.8 0.0 copy-done.3
  44.8 266.2 %solve.1 = (f32[192,128]{1,0:T(8,128)S(1)}, f32[1,192]{1,0:T(1,128)S(1)}) custom-call(f32[128,2048]{1,0:T(8,128)S(1)} %copy-done.3, f32[2048,128]{1,0:T(8,128)} %coup_ref.1, f32[8,56,128]{2,1,0:T(8,128)S(1)} %all-to-all-done.1.got_ref, f32[8,256]{1,0:T(8,128)S(1)} %get-tuple-element.7.slope_ref, f32[1,128]{1,0:T(1,128)S(1)} %dynamic-slice_bitcast_fusion.mass_ref), custom_call_target="tpu_custom_call" | custom-call | flops 10000000000 | bytes 100000000 | tf_op jit(solution)/shard_map/solve/pallas_call | solution.py:441
  311.0 0.6 copy.15
  311.6 0.6 copy.16
Async XLA Ops:
  0.6 37.0 %copy-start = (f32[2048]{0:T(1024)S(1)}, f32[2048]{0:T(1024)}, u32[]{:S(2)}) copy-start(f32[2048]{0:T(1024)} %param.18) | copy-start | bytes 24580
  2.0 20.6 %all-to-all-start = ((f32[128,1,128]{2,1,0:T(1,128)}), f32[128,1,128]{2,1,0:T(1,128)S(1)}, u32[]{:S(2)}, u32[]{:S(2)}) async-start(f32[128,1,128]{2,1,0:T(1,128)} %broadcast_in_dim.4), calls=%async_computation | async-start | bytes 131072 | tf_op jit(solution)/shard_map/all_to_all | solution.py:427
  22.5 1.3 copy-start.1
  23.8 1.3 copy-start.2
  25.1 0.8 copy-start.4
  25.9 0.7 copy-start.5
  26.6 0.7 copy-start.6
  27.2 17.5 %copy-start.3 = (f32[128,2048]{1,0:T(8,128)S(1)}, f32[128,2048]{1,0:T(8,128)}, u32[]{:S(2)}) copy-start(f32[128,2048]{1,0:T(8,128)} %diag_ref.1) | copy-start | bytes 3145732
  34.3 10.5 %all-to-all-start.1 = ((f32[8,56,128]{2,1,0:T(8,128)}), f32[8,56,128]{2,1,0:T(8,128)S(1)}, u32[]{:S(2)}, u32[]{:S(2)}) async-start(f32[8,56,128]{2,1,0:T(8,128)} %get-tuple-element.6), calls=%async_computation.1 | async-start | bytes 458752 | tf_op jit(solution)/shard_map/all_to_all | solution.py:438

commit v3 on v2

--- a/solution.py
+++ b/solution.py
@@ -29,15 +29,14 @@
     return high, middle, x - high - middle
 
 
-def loads_kernel(nc, lam_ref, table_ref, stiff_ref, mass_ref, dofs_ref, slab_ref, var_ref,
-                 send_ref, slope_ref, mode_at, loads):
+def element_loads(nc, lam_ref, table_ref, stiff_ref, mass_ref, dofs_ref, slab_ref, var_ref,
+                  send_ref, slope_ref, mode_at, loads, matrices_here):
     ed, count = dofs_ref.shape
     lanes = table_ref.shape[1]
     cap = send_ref.shape[2]
-    per_slab = table_ref.shape[0] // nc
     lam = lam_ref[0]
     dofs, slab, var = dofs_ref[...], slab_ref[...], var_ref[...]
-    row_of = slab * per_slab + lax.shift_right_logical(dofs, 7)
+    row_of = lax.shift_right_logical(dofs, 7) * nc + slab
     lane_of = jnp.bitwise_and(dofs, lanes - 1)
     chunks = count // lanes
 
@@ -56,6 +55,7 @@
     for c in range(chunks):
         mode_at[:, c * lanes : (c + 1) * lanes] = found[c]
     modes = mode_at[...]
+    matrices_here()
     for i in range(ed):
         operator = stiff_ref[i] - lam * mass_ref[i]
         loads[i : i + 1, :] = -jnp.sum(operator * modes, axis=0, keepdims=True)
@@ -88,10 +88,11 @@
         send_ref[k, 2 * ed : 2 * ed + 8, :] = packed[5 * ed : 5 * ed + 8]
 
 
-def solve_kernel(nc, nb, diag_ref, coup_ref, got_ref, slope_ref, mass_ref, out_ref, slope_out,
+def solve_kernel(nc, nb, lam_ref, diag_ref, coup_ref, stiff_ref, emass_ref, dofs_ref, slab_ref, var_ref, mode_ref, mass_ref,
+                 out_ref, slope_out, stiff, emass, mode_tile, mode_chain, mode_group, table, mode_at, loads, send_ref, got_ref, slope_ref,
                  dbuf, cbuf, dsplit, csplit, spread_ref, rpart, rbuf, sl_chain, sl_band,
                  part, slots, piece, full, ybuf, xbuf,
-                 mat, own_send, relay_send, slc_send, slc_recv, slb_send, slb_recv, r_send, r_recv,
+                 el_sem, mc_send, mc_recv, mb_send, mb_recv, ex_send, ex_recv, mat, own_send, relay_send, slc_send, slc_recv, slb_send, slb_recv, r_send, r_recv,
                  rs_send, rs_recv, ag_send, ag_recv, out_send, out_recv):
     me, band = lax.axis_index("chain"), lax.axis_index("band")
     x_len = nc // 2
@@ -130,8 +131,13 @@
         to = (along_x(1), along_x(-1), sibling)[i]
         return remote((diag_ref, coup_ref)[which], blocks[which].at[me], own_send.at[which, i], mat.at[which, me], to, band)
 
+    stiff_load = pltpu.make_async_copy(stiff_ref, stiff, el_sem.at[0])
+    emass_load = pltpu.make_async_copy(emass_ref, emass, el_sem.at[1])
+    stiff_load.start()
+    emass_load.start()
     for which in range(2):
         each_block(which, lambda which=which: own_load(which).start())
+    mode_tile[...] = jnp.broadcast_to(mode_ref[...], mode_tile.shape)
 
     barrier = pltpu.get_barrier_semaphore()
     for r in range(1, nb):
@@ -140,43 +146,94 @@
         pl.semaphore_signal(barrier, inc=1, device_id=(lax.rem(me + r, nc), band), device_id_type=MESH)
     pl.semaphore_wait(barrier, nb + nc - 2)
 
-    def slope_chain_copy(to, source):
-        return remote(slope_ref, sl_chain.at[source], slc_send.at[to], slc_recv.at[source], to, band)
-
-    for r in range(1, nc):
-        slope_chain_copy(lax.rem(me + r, nc), me).start()
-    sl_chain[me] = slope_ref[...]
+    def mode_chain_copy(to, source):
+        return remote(mode_tile, mode_chain.at[source], mc_send.at[to], mc_recv.at[source], to, band)
+
+    for r in range(1, nc):
+        mode_chain_copy(lax.rem(me + r, nc), me).start()
+    mode_chain[me] = mode_tile[...]
 
     def send_own(which):
         for i in range(3):
             own_copy(which, i).start()
 
-    for which in range(2):
-        each_block(which, functools.partial(send_own, which))
-
-    def relay_copies(which, by):
+    pl.when(core == 0)(lambda: send_own(0))
+    for r in range(1, nc):
+        mode_chain_copy(me, lax.rem(me + r, nc)).wait_recv()
+    line = lax.broadcasted_iota(jnp.int32, (nc, cols), 0)
+    whole = jnp.zeros((nc, cols), F32)
+    for c in range(nc):
+        whole = jnp.where(line == c, mode_chain[c], whole)
+    mode_group[...] = whole
+
+    def at_rows(b):
+        return table.at[pl.ds(pl.multiple_of(b * nc, 8), nc), :]
+
+    def mode_band_copy(r):
+        to = lax.rem(band + r, nb)
+        return remote(mode_group, at_rows(band), mb_send.at[r], mb_recv.at[r], me, to)
+
+    def mode_band_arrival(r):
+        source = lax.rem(band - r + nb, nb)
+        return remote(mode_group, at_rows(source), mb_send.at[r], mb_recv.at[r], me, source)
+
+    for r in range(1, nb):
+        mode_band_copy(r).start()
+    table[pl.ds(pl.multiple_of(band * nc, 8), nc), :] = whole
+    for r in range(1, nb):
+        mode_band_arrival(r).wait_recv()
+
+    def matrices_here():
+        stiff_load.wait()
+        emass_load.wait()
+
+    element_loads(nc, lam_ref, table, stiff, emass, dofs_ref, slab_ref, var_ref, send_ref, slope_ref, mode_at, loads, matrices_here)
+
+    def element_copy(to, source):
+        return remote(send_ref.at[to], got_ref.at[source], ex_send.at[to], ex_recv.at[source], to, band)
+
+    def slope_chain_copy(to, source):
+        return remote(slope_ref, sl_chain.at[source], slc_send.at[to], slc_recv.at[source], to, band)
+
+    for r in range(1, nc):
+        element_copy(lax.rem(me + r, nc), me).start()
+        slope_chain_copy(lax.rem(me + r, nc), me).start()
+    sl_chain[me] = slope_ref[...]
+    got_ref[me] = send_ref[me]
+    pl.when(core == 1)(lambda: send_own(0))
+    each_block(1, lambda: send_own(1))
+    for r in range(1, nc):
+        element_copy(me, lax.rem(me + r, nc)).wait_recv()
+
+    def relay_on(which, by):
         slab = along_x(-by)
         block = blocks[which].at[slab]
-        on = remote(block, block, relay_send.at[which, by, 0], mat.at[which, slab], sibling, band)
-        further = remote(block, block, relay_send.at[which, by, 1], mat.at[which, slab], along_x(1 if by == 1 else -1), band)
-        return slab, on, further
-
-    def forwards(by):
-        return {1: core == 0, 3: core == 1}[by]
-
-    def relay(which, by):
-        slab, on, further = relay_copies(which, by)
-
-        def work():
-            pltpu.make_async_copy(blocks[which].at[slab], blocks[which].at[slab], mat.at[which, slab]).wait()
-            on.start()
-            if by != 2:
-                pl.when(forwards(by))(lambda: further.start())
-
+        return remote(block, block, relay_send.at[which, by, 0], mat.at[which, slab], sibling, band)
+
+    def relay_further(which, by):
+        slab = along_x(-by)
+        block = blocks[which].at[slab]
+        return remote(block, block, relay_send.at[which, by, 1], mat.at[which, slab], along_x(1 if by == 1 else -1), band)
+
+    def each_relayed(which, by, work):
         if which == 0:
             work()
         else:
-            pl.when(slab != 0)(work)
+            pl.when(along_x(-by) != 0)(work)
+
+    def forwards(by):
+        return {1: core == 0, 3: core == 1}[by]
+
+    def relay(which, by):
+        slab = along_x(-by)
+
+        def work():
+            pltpu.make_async_copy(blocks[which].at[slab], blocks[which].at[slab], mat.at[which, slab]).wait()
+            if by != 2:
+                pl.when(forwards(by))(lambda: relay_further(which, by).start())
+            relay_on(which, by).start()
+
+        each_relayed(which, by, work)
 
     def relay_farthest(which, k):
         pl.when(k == along_x(2))(lambda: relay(which, 2))
@@ -391,8 +448,11 @@
         out_copy(me, other).wait_recv()
         rhs_copy(other, me).wait_send()
         slope_chain_copy(other, me).wait_send()
+        mode_chain_copy(other, me).wait_send()
+        element_copy(other, me).wait_send()
     for r in range(1, nb):
         slope_band_copy(r).wait_send()
+        mode_band_copy(r).wait_send()
 
     def sent(which):
         for i in range(3):
@@ -401,17 +461,13 @@
     for which in range(2):
         each_block(which, functools.partial(sent, which))
         for by in (1, 2, 3):
-            slab, on, further = relay_copies(which, by)
-
-            def relayed(on=on, further=further, by=by):
-                on.wait_send()
+
+            def relayed(which=which, by=by):
+                relay_on(which, by).wait_send()
                 if by != 2:
-                    pl.when(forwards(by))(lambda: further.wait_send())
-
-            if which == 0:
-                relayed()
-            else:
-                pl.when(slab != 0)(relayed)
+                    pl.when(forwards(by))(lambda: relay_further(which, by).wait_send())
+
+            each_relayed(which, by, relayed)
 
 
 def on_device(nc, nb, diag_inverse, coupling, elem_stiff, elem_mass, elem_dofs, elem_slab, elem_var, mode, mass_mode, eigenvalue):
@@ -420,30 +476,28 @@
     ed, count = elem_dofs.shape
     cap = count // 4
     rows = VARS // nc
-    everyone = nc * nb
     padded = 256
     vmem = pl.BlockSpec(memory_space=pltpu.VMEM)
     anywhere = pl.BlockSpec(memory_space=pl.ANY)
-    table = lax.all_to_all(jnp.broadcast_to(mode[None, :], (everyone, cols)), ("chain", "band"), 0, 0, tiled=True)
-    send, slope = pl.pallas_call(
-        functools.partial(loads_kernel, nc),
-        out_shape=(jax.ShapeDtypeStruct((nc, 2 * ed + 8, cap), F32), jax.ShapeDtypeStruct((8, padded), F32)),
-        in_specs=[pl.BlockSpec(memory_space=pltpu.SMEM)] + [vmem] * 6,
-        out_specs=(vmem, vmem),
-        scratch_shapes=[pltpu.VMEM((ed, count), F32), pltpu.VMEM((ed, count), F32)],
-        compiler_params=pltpu.CompilerParams(vmem_limit_bytes=30 * 1024 * 1024),
-        cost_estimate=pl.CostEstimate(flops=2 * 10**9, bytes_accessed=10**7, transcendentals=0),
-        name="loads",
-    )(eigenvalue, table, elem_stiff, elem_mass, elem_dofs, elem_slab.reshape(1, count), elem_var.reshape(1, count))
-    got = lax.all_to_all(send, "chain", 0, 0, tiled=True)
     own_mass = lax.dynamic_slice_in_dim(mass_mode, band * cols, cols)[None, :]
     dma = pltpu.SemaphoreType.DMA
     eigvec_slope, eigval_slope = pl.pallas_call(
         functools.partial(solve_kernel, nc, nb),
         out_shape=(jax.ShapeDtypeStruct((VARS, cols), F32), jax.ShapeDtypeStruct((1, VARS), F32)),
-        in_specs=[anywhere, anywhere, vmem, vmem, vmem],
+        in_specs=[pl.BlockSpec(memory_space=pltpu.SMEM)] + [anywhere] * 4 + [vmem] * 5,
         out_specs=(vmem, vmem),
         scratch_shapes=[
+            pltpu.VMEM((ed, ed, count), F32),
+            pltpu.VMEM((ed, ed, count), F32),
+            pltpu.VMEM((8, cols), F32),
+            pltpu.VMEM((nc, 8, cols), F32),
+            pltpu.VMEM((nc, cols), F32),
+            pltpu.VMEM((nc * nb, cols), F32),
+            pltpu.VMEM((ed, count), F32),
+            pltpu.VMEM((ed, count), F32),
+            pltpu.VMEM((nc, 2 * ed + 8, cap), F32),
+            pltpu.VMEM((nc, 2 * ed + 8, cap), F32),
+            pltpu.VMEM((8, padded), F32),
             pltpu.VMEM((nc, cols, width), F32),
             pltpu.VMEM((nc, width, cols), F32),
             pltpu.VMEM((nc, 2 * cols, width), BF16),
@@ -459,6 +513,7 @@
             pltpu.VMEM((rows, width), F32),
             pltpu.VMEM((nc, rows, cols), F32),
             pltpu.VMEM((nc, rows, cols), F32),
+            dma((2,)), dma((nc,)), dma((nc,)), dma((nb,)), dma((nb,)), dma((nc,)), dma((nc,)),
             dma((2, nc)), dma((2, 3)), dma((2, 4, 2)),
             dma((nc,)), dma((nc,)), dma((nb,)), dma((nb,)), dma((nc,)), dma((nc,)),
             dma((nb,)), dma((nb,)), dma((nb,)), dma((nb,)), dma((nc,)), dma((nc,)),
@@ -466,7 +521,8 @@
         compiler_params=pltpu.CompilerParams(collective_id=0, has_side_effects=True, vmem_limit_bytes=52 * 1024 * 1024),
         cost_estimate=pl.CostEstimate(flops=10**10, bytes_accessed=10**8, transcendentals=0),
         name="solve",
-    )(diag_inverse, coupling, got, slope, own_mass)
+    )(eigenvalue, diag_inverse, coupling, elem_stiff, elem_mass, elem_dofs, elem_slab.reshape(1, count),
+      elem_var.reshape(1, count), mode[None, :], own_mass)
     return eigvec_slope, eigval_slope.reshape(VARS)
 
 

time: 313 us -> 285 us (0.911)
  waiting for transfers between devices: 15.8 us -> 0 us
  starting transfers between devices: 14.5 us -> 0 us
  Pallas kernels: 273 us -> 278 us
    all_to_all x2 -> x0, waiting for transfers between devices: 15.8 us -> none  [the longest x1 8.76 us: on_device(): lax.all_to_all(jnp.broadcast_to(mode[None, :], (everyone, cols)), ('chain...]
    all_to_all x2 -> x0, starting transfers between devices: 14.5 us -> none  [the longest x1 11.1 us: on_device(): lax.all_to_all(jnp.broadcast_to(mode[None, :], (everyone, cols)), ('chain...]
    pallas_call x1, Pallas kernels: 266 us -> 278 us  [on_device(): pl.pallas_call(functools.partial(solve_kernel, nc, nb), out_shape=(jax.Sh...]
    pallas_call x1 -> x0, Pallas kernels: 7.02 us -> none  [on_device(): pl.pallas_call(functools.partial(loads_kernel, nc), out_shape=(jax.ShapeD...]
  transfers between devices with their start and end apart: 2 -> 0, of which waited for: 2 -> 0; matrix products, arithmetic and copies ran while one was open for 0% -> 0% of each run, Pallas kernels for 0% -> 0%
where the time goes in v3:
time: 285 us
  Pallas kernels  278 us (98%)
  local copies, waits for them, and re-layouts  5.36 us (2%)
    pallas_call x1, Pallas kernels, on_device(): pl.pallas_call(functools.partial(solve_kernel, nc, nb), out_shape=(jax.Sh...  278 us

profile of v3, /device:TPU:0, one launch (start us, length us, event | category | flops | bytes accessed | tf_op | source)
XLA Modules:
  0.0 284.7 jit_solution(4463568015744611586)
XLA Ops:
  0.6 0.0 copy-start
  1.3 0.0 copy-done
  1.3 0.1 dynamic-slice_bitcast_fusion.mass_ref
  1.4 0.0 copy-start.1
  1.4 1.2 copy-done.1
  2.6 0.0 copy-start.2
  2.6 0.8 copy-done.2
  3.4 0.0 copy-start.3
  3.4 0.7 copy-done.3
  4.1 0.0 copy-start.4
  4.1 0.7 copy-done.4
  4.8 0.0 copy-start.5
  4.8 0.7 copy-done.5
  5.5 278.0 %solve.1 = (f32[192,128]{1,0:T(8,128)S(1)}, f32[1,192]{1,0:T(1,128)S(1)}) custom-call(f32[1]{0:T(128)S(6)} %copy.14.lam_ref, f32[128,2048]{1,0:T(8,128)S(1)} %copy-done.1, f32[2048,128]{1,0:T(8,128)} %coup_ref.1, f32[24,24,512]{2,1,0:T(8,128)} %stiff_ref.1, f32[24,24,512]{2,1,0:T(8,128)} %emass_ref.1, s32[24,512]{1,0:T(8,128)S(1)} %copy-done.2, ...), custom_call_target="tpu_custom_call" | custom-call | flops 10000000000 | bytes 100000000 | tf_op jit(solution)/shard_map/solve/pallas_call | solution.py:484
  283.4 0.6 copy.15
  284.1 0.6 copy.16
Async XLA Ops:
  0.6 0.7 copy-start
  1.4 1.2 copy-start.1
  2.6 0.8 copy-start.2
  3.4 0.7 copy-start.3
  4.1 0.7 copy-start.4
  4.8 0.7 copy-start.5

commit v4 on v3

--- a/solution.py
+++ b/solution.py
@@ -1,4 +1,5 @@
 import functools
+import math
 
 import jax
 import jax.numpy as jnp
@@ -90,9 +91,9 @@
 
 def solve_kernel(nc, nb, lam_ref, diag_ref, coup_ref, stiff_ref, emass_ref, dofs_ref, slab_ref, var_ref, mode_ref, mass_ref,
                  out_ref, slope_out, stiff, emass, mode_tile, mode_chain, mode_group, table, mode_at, loads, send_ref, got_ref, slope_ref,
-                 dbuf, cbuf, dsplit, csplit, spread_ref, rpart, rbuf, sl_chain, sl_band,
+                 dbuf, cbuf, dsplit, csplit, spread_ref, rpart, rbuf, sl_chain, sl_band, outer,
                  part, slots, piece, full, ybuf, xbuf,
-                 el_sem, mc_send, mc_recv, mb_send, mb_recv, ex_send, ex_recv, mat, own_send, relay_send, slc_send, slc_recv, slb_send, slb_recv, r_send, r_recv,
+                 el_sem, mc_send, mc_recv, mb_send, mb_recv, ex_send, ex_recv, mat, own_send, relay_send, slc_send, slc_recv, slb_send, slb_recv, r_send, r_recv, rp_send, rp_recv,
                  rs_send, rs_recv, ag_send, ag_recv, out_send, out_recv):
     me, band = lax.axis_index("chain"), lax.axis_index("band")
     x_len = nc // 2
@@ -108,6 +109,17 @@
     def at_band(b):
         return pl.ds(pl.multiple_of(b * cols, cols), cols)
 
+    side = math.isqrt(nb)
+    hops = lambda r: min(r // side, side - r // side) + min(r % side, side - r % side)
+    others = sorted(range(1, nb), key=lambda r: (-hops(r), r))
+    band_z, band_y = band // side, lax.rem(band, side)
+
+    def band_to(r):
+        return lax.rem(band_z + r // side, side) * side + lax.rem(band_y + r % side, side)
+
+    def band_from(r):
+        return lax.rem(band_z + side - r // side, side) * side + lax.rem(band_y + side - r % side, side)
+
     def at_group(c):
         return pl.ds(pl.multiple_of(c * rows, 8), rows)
 
@@ -137,11 +149,12 @@
     emass_load.start()
     for which in range(2):
         each_block(which, lambda which=which: own_load(which).start())
-    mode_tile[...] = jnp.broadcast_to(mode_ref[...], mode_tile.shape)
+    line = lax.broadcasted_iota(jnp.int32, mode_tile.shape, 0)
+    mode_tile[...] = jnp.where(line == 0, mode_ref[...], jnp.where(line == 1, mass_ref[...], 0.0))
 
     barrier = pltpu.get_barrier_semaphore()
     for r in range(1, nb):
-        pl.semaphore_signal(barrier, inc=1, device_id=(me, lax.rem(band + r, nb)), device_id_type=MESH)
+        pl.semaphore_signal(barrier, inc=1, device_id=(me, band_to(r)), device_id_type=MESH)
     for r in range(1, nc):
         pl.semaphore_signal(barrier, inc=1, device_id=(lax.rem(me + r, nc), band), device_id_type=MESH)
     pl.semaphore_wait(barrier, nb + nc - 2)
@@ -157,27 +170,28 @@
         for i in range(3):
             own_copy(which, i).start()
 
-    pl.when(core == 0)(lambda: send_own(0))
+    pl.when(me != 1)(lambda: send_own(0))
+    pl.when(me == 1)(lambda: send_own(1))
     for r in range(1, nc):
         mode_chain_copy(me, lax.rem(me + r, nc)).wait_recv()
     line = lax.broadcasted_iota(jnp.int32, (nc, cols), 0)
     whole = jnp.zeros((nc, cols), F32)
     for c in range(nc):
-        whole = jnp.where(line == c, mode_chain[c], whole)
+        whole = jnp.where(line == c, mode_chain[c, 0:1, :], whole)
     mode_group[...] = whole
 
     def at_rows(b):
         return table.at[pl.ds(pl.multiple_of(b * nc, 8), nc), :]
 
     def mode_band_copy(r):
-        to = lax.rem(band + r, nb)
+        to = band_to(r)
         return remote(mode_group, at_rows(band), mb_send.at[r], mb_recv.at[r], me, to)
 
     def mode_band_arrival(r):
-        source = lax.rem(band - r + nb, nb)
+        source = band_from(r)
         return remote(mode_group, at_rows(source), mb_send.at[r], mb_recv.at[r], me, source)
 
-    for r in range(1, nb):
+    for r in others:
         mode_band_copy(r).start()
     table[pl.ds(pl.multiple_of(band * nc, 8), nc), :] = whole
     for r in range(1, nb):
@@ -188,6 +202,39 @@
         emass_load.wait()
 
     element_loads(nc, lam_ref, table, stiff, emass, dofs_ref, slab_ref, var_ref, send_ref, slope_ref, mode_at, loads, matrices_here)
+
+    def relay_on(which, by):
+        slab = along_x(-by)
+        block = blocks[which].at[slab]
+        return remote(block, block, relay_send.at[which, by, 0], mat.at[which, slab], sibling, band)
+
+    def relay_further(which, by):
+        slab = along_x(-by)
+        block = blocks[which].at[slab]
+        return remote(block, block, relay_send.at[which, by, 1], mat.at[which, slab], along_x(1 if by == 1 else -1), band)
+
+    def each_relayed(which, by, work):
+        if which == 0:
+            work()
+        else:
+            pl.when(along_x(-by) != 0)(work)
+
+    def forwards(by):
+        return {1: core == 0, 3: core == 1}[by]
+
+    def relay(which, by):
+        slab = along_x(-by)
+
+        def work():
+            pltpu.make_async_copy(blocks[which].at[slab], blocks[which].at[slab], mat.at[which, slab]).wait()
+            if by != 2:
+                pl.when(forwards(by))(lambda: relay_further(which, by).start())
+            relay_on(which, by).start()
+
+        each_relayed(which, by, work)
+
+    def relay_farthest(which, k):
+        pl.when(k == along_x(2))(lambda: relay(which, 2))
 
     def element_copy(to, source):
         return remote(send_ref.at[to], got_ref.at[source], ex_send.at[to], ex_recv.at[source], to, band)
@@ -200,43 +247,17 @@
         slope_chain_copy(lax.rem(me + r, nc), me).start()
     sl_chain[me] = slope_ref[...]
     got_ref[me] = send_ref[me]
-    pl.when(core == 1)(lambda: send_own(0))
-    each_block(1, lambda: send_own(1))
+    pl.when(core == 0)(lambda: relay(0, 1))
+
+    @pl.when(core == 1)
+    def _():
+        pl.when(along_x(1) != 1)(lambda: relay(0, 3))
+        pl.when(along_x(1) == 1)(lambda: relay(1, 3))
+
+    pl.when(me == 1)(lambda: send_own(0))
+    pl.when((me != 0) & (me != 1))(lambda: send_own(1))
     for r in range(1, nc):
         element_copy(me, lax.rem(me + r, nc)).wait_recv()
-
-    def relay_on(which, by):
-        slab = along_x(-by)
-        block = blocks[which].at[slab]
-        return remote(block, block, relay_send.at[which, by, 0], mat.at[which, slab], sibling, band)
-
-    def relay_further(which, by):
-        slab = along_x(-by)
-        block = blocks[which].at[slab]
-        return remote(block, block, relay_send.at[which, by, 1], mat.at[which, slab], along_x(1 if by == 1 else -1), band)
-
-    def each_relayed(which, by, work):
-        if which == 0:
-            work()
-        else:
-            pl.when(along_x(-by) != 0)(work)
-
-    def forwards(by):
-        return {1: core == 0, 3: core == 1}[by]
-
-    def relay(which, by):
-        slab = along_x(-by)
-
-        def work():
-            pltpu.make_async_copy(blocks[which].at[slab], blocks[which].at[slab], mat.at[which, slab]).wait()
-            if by != 2:
-                pl.when(forwards(by))(lambda: relay_further(which, by).start())
-            relay_on(which, by).start()
-
-        each_relayed(which, by, work)
-
-    def relay_farthest(which, k):
-        pl.when(k == along_x(2))(lambda: relay(which, 2))
 
     cap = got_ref.shape[2]
     ed = (got_ref.shape[1] - 8) // 2
@@ -246,6 +267,20 @@
     variable = lax.broadcasted_iota(jnp.int32, (nvars, cap), 0)
     matches = [(variable == got_ref[s, 2 * ed : 2 * ed + 1, :].astype(jnp.int32)).astype(F32).astype(BF16) for s in range(nc)]
     matches = jnp.concatenate(matches + matches, axis=1)
+
+    def rhs_copy(to, source):
+        return remote(rpart.at[at_group(to), :], rbuf.at[source], r_send.at[to], r_recv.at[source], to, band)
+
+    def rhs_part_copy(to, n):
+        at = pl.ds(pl.multiple_of(n * block, block), block)
+        return remote(rpart.at[at_group(to), at], rbuf.at[0, :, at], rp_send.at[to, n], rp_recv.at[n], to, band)
+
+    def send_rhs():
+        for r in range(1, nc):
+            rhs_copy(lax.rem(me + r, nc), me).start()
+
+    def rhs_wait(k):
+        pl.when(k != me)(lambda: rhs_copy(me, k).wait_recv())
 
     def one_block(n, carry):
         def one_source(s, inner):
@@ -266,9 +301,17 @@
         lax.fori_loop(0, nc, one_source, 0)
         at = pl.ds(pl.multiple_of(n * block, block), block)
         rpart[:, at] = lax.dot_general(matches, spread_ref[...], nt, preferred_element_type=F32)
+
+        @pl.when(me == 0)
+        def _():
+            for r in range(1, nc):
+                rhs_part_copy(r, n).start()
+
         return carry
 
     lax.fori_loop(0, width // block, one_block, 0)
+
+    rbuf[me] = rpart[at_group(me), :]
 
     for r in range(1, nc):
         slope_chain_copy(me, lax.rem(me + r, nc)).wait_recv()
@@ -277,81 +320,87 @@
         total = total + sl_chain[c]
 
     def slope_band_copy(r):
-        to = lax.rem(band + r, nb)
+        to = band_to(r)
         return remote(sl_band.at[band], sl_band.at[band], slb_send.at[r], slb_recv.at[r], me, to)
 
     def slope_band_arrival(r):
-        source = lax.rem(band - r + nb, nb)
+        source = band_from(r)
         return remote(sl_band.at[source], sl_band.at[source], slb_send.at[r], slb_recv.at[r], me, source)
 
     sl_band[band] = total
-    for r in range(1, nb):
+    for r in others:
         slope_band_copy(r).start()
-    for by in (1, 3):
-        relay(0, by)
-    for r in range(1, nb):
-        slope_band_arrival(r).wait_recv()
-    total = sl_band[0]
-    for b in range(1, nb):
-        total = total + sl_band[b]
-    slope_out[...] = total[0:1, :nvars]
-    line = lax.broadcasted_iota(jnp.int32, total.shape, 0)
-    high, middle, low = three_way(total)
-    slope_terms = jnp.where((line == 0) | (line == 3) | (line == 5), high, 0.0)
-    slope_terms = jnp.where((line == 1) | (line == 4), middle, jnp.where(line == 2, low, slope_terms))
-    line = lax.broadcasted_iota(jnp.int32, (8, cols), 0)
-    high, middle, low = three_way(jnp.broadcast_to(mass_ref[...], (8, cols)))
-    mass_terms = jnp.where(line < 3, high, jnp.where(line < 5, middle, jnp.where(line == 5, low, 0.0)))
-    outer = lax.dot_general(slope_terms.astype(BF16), mass_terms.astype(BF16), (((0,), (0,)), ((), ())), preferred_element_type=F32)
-    rpart[:, at_band(band)] = rpart[:, at_band(band)] + outer[:nvars]
-
-    def rhs_copy(to, source):
-        return remote(rpart.at[at_group(to), :], rbuf.at[source], r_send.at[to], r_recv.at[source], to, band)
-
-    for r in range(1, nc):
-        rhs_copy(lax.rem(me + r, nc), me).start()
-    rbuf[me] = rpart[at_group(me), :]
-    for by in (1, 3):
-        relay(1, by)
-
-    def rhs_wait(k):
-        pl.when(k != me)(lambda: rhs_copy(me, k).wait_recv())
+
+    def slope_term():
+        for r in range(1, nb):
+            slope_band_arrival(r).wait_recv()
+        total = sl_band[0]
+        for b in range(1, nb):
+            total = total + sl_band[b]
+        slope_out[...] = total[0:1, :nvars]
+        line = lax.broadcasted_iota(jnp.int32, total.shape, 0)
+        high, middle, low = three_way(total)
+        slope_terms = jnp.where((line == 0) | (line == 3) | (line == 5), high, 0.0)
+        slope_terms = jnp.where((line == 1) | (line == 4), middle, jnp.where(line == 2, low, slope_terms))
+        line = lax.broadcasted_iota(jnp.int32, (8, cols), 0)
+        for k in range(nc):
+            high, middle, low = three_way(jnp.broadcast_to(mode_chain[k, 1:2, :], (8, cols)))
+            mass_terms = jnp.where(line < 3, high, jnp.where(line < 5, middle, jnp.where(line == 5, low, 0.0)))
+            outer[k] = lax.dot_general(slope_terms.astype(BF16), mass_terms.astype(BF16), (((0,), (0,)), ((), ())), preferred_element_type=F32)
+
+    @pl.when(core == 0)
+    def _():
+        relay(1, 1)
+        relay(0, 3)
+        relay(1, 3)
+
+    @pl.when(core == 1)
+    def _():
+        pl.when(along_x(1) != 1)(lambda: relay(1, 3))
+        pl.when(along_x(1) == 1)(lambda: relay(0, 3))
+        relay(0, 1)
+        relay(1, 1)
+
 
     def rs_copy(r):
-        to = lax.rem(band + r, nb)
+        to = band_to(r)
         return remote(part.at[:, at_band(to)], slots.at[r], rs_send.at[r], rs_recv.at[r], me, to)
 
     def ag_copy(r):
-        to = lax.rem(band + r, nb)
+        to = band_to(r)
         return remote(piece, full.at[:, at_band(band)], ag_send.at[r], ag_recv.at[r], me, to)
 
     def ag_arrival(r):
-        source = lax.rem(band - r + nb, nb)
+        source = band_from(r)
         return remote(piece, full.at[:, at_band(source)], ag_send.at[r], ag_recv.at[r], me, source)
 
     def reduce_start():
-        for r in range(1, nb):
+        for r in others:
             rs_copy(r).start()
 
-    def reduce_end():
-        total = part[:, at_band(band)]
-        for r in range(1, nb):
+    def reduce_end(own):
+        total = own
+        for r in reversed(others):
             rs_copy(r).wait_recv()
             total = total + slots[r]
-        for r in range(1, nb):
+        return total
+
+    def reduce_sent():
+        for r in others:
             rs_copy(r).wait_send()
-        return total
 
     def gather_start(value):
         piece[...] = value
-        for r in range(1, nb):
+        for r in others:
             ag_copy(r).start()
         full[:, at_band(band)] = value
 
     def gather_end():
-        for r in range(1, nb):
+        for r in reversed(others):
             ag_arrival(r).wait_recv()
-        for r in range(1, nb):
+
+    def gather_sent():
+        for r in others:
             ag_copy(r).wait_send()
 
     def block_wait(which, k):
@@ -381,16 +430,25 @@
         wide = lax.dot_general(both, weights, dims, preferred_element_type=F32)
         return wide[:rows] + wide[rows:]
 
-    rhs_wait(0)
+    @pl.when(me != 0)
+    def _():
+        for n in range(width // block):
+            rhs_part_copy(me, n).wait_recv()
+
     part[...] = rbuf[0]
-    relay_farthest(0, 0)
+    pl.when(me == 1)(send_rhs)
 
     def forward(k, carry):
         reduce_start()
+        pl.when(me == k + 2)(send_rhs)
+        pl.when(k > 0)(gather_sent)
+        pl.when(k == 0)(lambda: relay_farthest(0, 0))
+        pl.when(k == 0)(slope_term)
         relay_farthest(0, k + 1)
         relay_farthest(1, k + 1)
         split_diag(k)
-        gather_start(reduce_end())
+        gather_start(reduce_end(part[:, at_band(band)] + outer[k, at_group(me), :]))
+        reduce_sent()
 
         @pl.when(k + 1 < nc)
         def _():
@@ -416,8 +474,10 @@
         k = nc - 1 - step
         part[...] = spread(ybuf[k] - coupled, dsplit[k], nn)
         reduce_start()
-        total = reduce_end()
+        gather_sent()
+        total = reduce_end(part[:, at_band(band)])
         gather_start(total)
+        reduce_sent()
         xbuf[k] = total
 
         @pl.when(k != me)
@@ -434,7 +494,8 @@
     coupled = lax.fori_loop(0, nc - 1, backward, jnp.zeros((rows, cols), F32))
     part[...] = spread(ybuf[0] - coupled, dsplit[0], nn)
     reduce_start()
-    total = reduce_end()
+    gather_sent()
+    total = reduce_end(part[:, at_band(band)])
     xbuf[0] = total
     pl.when(me != 0)(lambda: out_copy(0, me).start())
 
@@ -446,10 +507,17 @@
         other = lax.rem(me + r, nc)
         out_copy(other, me).wait_send()
         out_copy(me, other).wait_recv()
-        rhs_copy(other, me).wait_send()
+        pl.when(me != 0)(lambda other=other: rhs_copy(other, me).wait_send())
+
+        @pl.when(me == 0)
+        def _():
+            for n in range(width // block):
+                rhs_part_copy(other, n).wait_send()
+
         slope_chain_copy(other, me).wait_send()
         mode_chain_copy(other, me).wait_send()
         element_copy(other, me).wait_send()
+    reduce_sent()
     for r in range(1, nb):
         slope_band_copy(r).wait_send()
         mode_band_copy(r).wait_send()
@@ -507,6 +575,7 @@
             pltpu.VMEM((nc, rows, width), F32),
             pltpu.VMEM((nc, 8, padded), F32),
             pltpu.VMEM((nb, 8, padded), F32),
+            pltpu.VMEM((nc, padded, cols), F32),
             pltpu.VMEM((rows, width), F32),
             pltpu.VMEM((nb, rows, cols), F32),
             pltpu.VMEM((rows, cols), F32),
@@ -516,6 +585,7 @@
             dma((2,)), dma((nc,)), dma((nc,)), dma((nb,)), dma((nb,)), dma((nc,)), dma((nc,)),
             dma((2, nc)), dma((2, 3)), dma((2, 4, 2)),
             dma((nc,)), dma((nc,)), dma((nb,)), dma((nb,)), dma((nc,)), dma((nc,)),
+            dma((nc, 8)), dma((8,)),
             dma((nb,)), dma((nb,)), dma((nb,)), dma((nb,)), dma((nc,)), dma((nc,)),
         ],
         compiler_params=pltpu.CompilerParams(collective_id=0, has_side_effects=True, vmem_limit_bytes=52 * 1024 * 1024),

time: 285 us -> 264 us (0.926)
  Pallas kernels: 278 us -> 257 us
    pallas_call x1, Pallas kernels: 278 us -> 257 us  [on_device(): pl.pallas_call(functools.partial(solve_kernel, nc, nb), out_shape=(jax.Sh...]
where the time goes in v4:
time: 264 us; the launch traced here: 263 us
  Pallas kernels  257 us (97%)
  local copies, waits for them, and re-layouts  5.36 us (2%)
    pallas_call x1, Pallas kernels, on_device(): pl.pallas_call(functools.partial(solve_kernel, nc, nb), out_shape=(jax.Sh...  257 us
    unnamed x14, local copies, waits for them, and re-layouts  5.28 us

profile of v4, /device:TPU:0, one launch (start us, length us, event | category | flops | bytes accessed | tf_op | source)
XLA Modules:
  0.0 263.4 jit_solution(15422616671143951484)
XLA Ops:
  0.6 0.0 copy-start
  1.3 0.0 copy-done
  1.3 0.1 dynamic-slice_bitcast_fusion.mass_ref
  1.4 0.0 copy-start.1
  1.4 1.2 copy-done.1
  2.6 0.0 copy-start.2
  2.6 0.8 copy-done.2
  3.4 0.0 copy-start.3
  3.4 0.7 copy-done.3
  4.1 0.0 copy-start.4
  4.1 0.7 copy-done.4
  4.8 0.0 copy-start.5
  4.8 0.7 copy-done.5
  5.5 256.7 %solve.1 = (f32[192,128]{1,0:T(8,128)S(1)}, f32[1,192]{1,0:T(1,128)S(1)}) custom-call(f32[1]{0:T(128)S(6)} %copy.14.lam_ref, f32[128,2048]{1,0:T(8,128)S(1)} %copy-done.1, f32[2048,128]{1,0:T(8,128)} %coup_ref.1, f32[24,24,512]{2,1,0:T(8,128)} %stiff_ref.1, f32[24,24,512]{2,1,0:T(8,128)} %emass_ref.1, s32[24,512]{1,0:T(8,128)S(1)} %copy-done.2, ...), custom_call_target="tpu_custom_call" | custom-call | flops 10000000000 | bytes 100000000 | tf_op jit(solution)/shard_map/solve/pallas_call | solution.py:552
  262.2 0.6 copy.15
  262.8 0.6 copy.16
Async XLA Ops:
  0.6 0.7 copy-start
  1.4 1.2 copy-start.1
  2.6 0.8 copy-start.2
  3.4 0.7 copy-start.3
  4.1 0.7 copy-start.4
  4.8 0.7 copy-start.5

commit v5 on v4

--- a/solution.py
+++ b/solution.py
@@ -89,11 +89,11 @@
         send_ref[k, 2 * ed : 2 * ed + 8, :] = packed[5 * ed : 5 * ed + 8]
 
 
-def solve_kernel(nc, nb, lam_ref, diag_ref, coup_ref, stiff_ref, emass_ref, dofs_ref, slab_ref, var_ref, mode_ref, mass_ref,
-                 out_ref, slope_out, stiff, emass, mode_tile, mode_chain, mode_group, table, mode_at, loads, send_ref, got_ref, slope_ref,
-                 dbuf, cbuf, dsplit, csplit, spread_ref, rpart, rbuf, sl_chain, sl_band, outer,
+def solve_kernel(nc, nb, lam_ref, diag_ref, coup_ref, stiff_ref, emass_ref, dofs_in, slab_in, var_in, mode_in, mass_in,
+                 out_ref, slope_out, dofs_ref, slab_ref, var_ref, mode_ref, mass_ref, stiff, emass, mode_tile, mode_chain, mode_group, table, mode_at, loads, send_ref, got_ref, slope_ref,
+                 dbuf, cbuf, dsplit, csplit, spread_ref, rpart, rslots, rsum, rpiece, sl_chain, sl_band, outer,
                  part, slots, piece, full, ybuf, xbuf,
-                 el_sem, mc_send, mc_recv, mb_send, mb_recv, ex_send, ex_recv, mat, own_send, relay_send, slc_send, slc_recv, slb_send, slb_recv, r_send, r_recv, rp_send, rp_recv,
+                 el_sem, mc_send, mc_recv, mb_send, mb_recv, ex_send, ex_recv, mat, own_send, relay_send, slc_send, slc_recv, slb_send, slb_recv, r_send, r_recv, rq_send, rq_recv,
                  rs_send, rs_recv, ag_send, ag_recv, out_send, out_recv):
     me, band = lax.axis_index("chain"), lax.axis_index("band")
     x_len = nc // 2
@@ -143,12 +143,18 @@
         to = (along_x(1), along_x(-1), sibling)[i]
         return remote((diag_ref, coup_ref)[which], blocks[which].at[me], own_send.at[which, i], mat.at[which, me], to, band)
 
+    small = ((mode_in, mode_ref), (mass_in, mass_ref), (dofs_in, dofs_ref), (slab_in, slab_ref), (var_in, var_ref))
+    small_loads = [pltpu.make_async_copy(src, dst, el_sem.at[2 + i]) for i, (src, dst) in enumerate(small)]
+    for load in small_loads:
+        load.start()
     stiff_load = pltpu.make_async_copy(stiff_ref, stiff, el_sem.at[0])
     emass_load = pltpu.make_async_copy(emass_ref, emass, el_sem.at[1])
     stiff_load.start()
     emass_load.start()
     for which in range(2):
         each_block(which, lambda which=which: own_load(which).start())
+    for load in small_loads:
+        load.wait()
     line = lax.broadcasted_iota(jnp.int32, mode_tile.shape, 0)
     mode_tile[...] = jnp.where(line == 0, mode_ref[...], jnp.where(line == 1, mass_ref[...], 0.0))
 
@@ -159,19 +165,81 @@
         pl.semaphore_signal(barrier, inc=1, device_id=(lax.rem(me + r, nc), band), device_id_type=MESH)
     pl.semaphore_wait(barrier, nb + nc - 2)
 
-    def mode_chain_copy(to, source):
-        return remote(mode_tile, mode_chain.at[source], mc_send.at[to], mc_recv.at[source], to, band)
-
-    for r in range(1, nc):
-        mode_chain_copy(lax.rem(me + r, nc), me).start()
-    mode_chain[me] = mode_tile[...]
-
     def send_own(which):
         for i in range(3):
             own_copy(which, i).start()
 
-    pl.when(me != 1)(lambda: send_own(0))
-    pl.when(me == 1)(lambda: send_own(1))
+    def relay_on(which, by):
+        slab = along_x(-by)
+        block = blocks[which].at[slab]
+        return remote(block, block, relay_send.at[which, by, 0], mat.at[which, slab], sibling, band)
+
+    def relay_further(which, by):
+        slab = along_x(-by)
+        block = blocks[which].at[slab]
+        return remote(block, block, relay_send.at[which, by, 1], mat.at[which, slab], along_x(1 if by == 1 else -1), band)
+
+    def each_relayed(which, by, work):
+        if which == 0:
+            work()
+        else:
+            pl.when(along_x(-by) != 0)(work)
+
+    def forwards(by):
+        return {1: core == 0, 3: core == 1}[by]
+
+    def relay(which, by):
+        slab = along_x(-by)
+
+        def work():
+            pltpu.make_async_copy(blocks[which].at[slab], blocks[which].at[slab], mat.at[which, slab]).wait()
+            if by != 2:
+                pl.when(forwards(by))(lambda: relay_further(which, by).start())
+            relay_on(which, by).start()
+
+        each_relayed(which, by, work)
+
+    def relay_farthest(which, k):
+        pl.when(k == along_x(2))(lambda: relay(which, 2))
+
+    def first_sends():
+        pl.when(me != 1)(lambda: send_own(0))
+        pl.when(me == 1)(lambda: send_own(1))
+
+    def second_sends():
+        pl.when(me == 1)(lambda: send_own(0))
+        pl.when((me != 0) & (me != 1))(lambda: send_own(1))
+
+    def first_relays():
+        pl.when(core == 0)(lambda: relay(0, 1))
+
+        @pl.when(core == 1)
+        def _():
+            pl.when(along_x(1) != 1)(lambda: relay(0, 3))
+            pl.when(along_x(1) == 1)(lambda: relay(1, 3))
+
+    def second_relays():
+        @pl.when(core == 0)
+        def _():
+            relay(1, 1)
+            relay(0, 3)
+            relay(1, 3)
+
+        @pl.when(core == 1)
+        def _():
+            pl.when(along_x(1) != 1)(lambda: relay(1, 3))
+            pl.when(along_x(1) == 1)(lambda: relay(0, 3))
+            relay(0, 1)
+            relay(1, 1)
+
+    def mode_chain_copy(to, source):
+        return remote(mode_tile, mode_chain.at[source], mc_send.at[to], mc_recv.at[source], to, band)
+
+    for r in range(1, nc):
+        mode_chain_copy(lax.rem(me + r, nc), me).start()
+    mode_chain[me] = mode_tile[...]
+
+    first_sends()
     for r in range(1, nc):
         mode_chain_copy(me, lax.rem(me + r, nc)).wait_recv()
     line = lax.broadcasted_iota(jnp.int32, (nc, cols), 0)
@@ -203,39 +271,6 @@
 
     element_loads(nc, lam_ref, table, stiff, emass, dofs_ref, slab_ref, var_ref, send_ref, slope_ref, mode_at, loads, matrices_here)
 
-    def relay_on(which, by):
-        slab = along_x(-by)
-        block = blocks[which].at[slab]
-        return remote(block, block, relay_send.at[which, by, 0], mat.at[which, slab], sibling, band)
-
-    def relay_further(which, by):
-        slab = along_x(-by)
-        block = blocks[which].at[slab]
-        return remote(block, block, relay_send.at[which, by, 1], mat.at[which, slab], along_x(1 if by == 1 else -1), band)
-
-    def each_relayed(which, by, work):
-        if which == 0:
-            work()
-        else:
-            pl.when(along_x(-by) != 0)(work)
-
-    def forwards(by):
-        return {1: core == 0, 3: core == 1}[by]
-
-    def relay(which, by):
-        slab = along_x(-by)
-
-        def work():
-            pltpu.make_async_copy(blocks[which].at[slab], blocks[which].at[slab], mat.at[which, slab]).wait()
-            if by != 2:
-                pl.when(forwards(by))(lambda: relay_further(which, by).start())
-            relay_on(which, by).start()
-
-        each_relayed(which, by, work)
-
-    def relay_farthest(which, k):
-        pl.when(k == along_x(2))(lambda: relay(which, 2))
-
     def element_copy(to, source):
         return remote(send_ref.at[to], got_ref.at[source], ex_send.at[to], ex_recv.at[source], to, band)
 
@@ -247,71 +282,10 @@
         slope_chain_copy(lax.rem(me + r, nc), me).start()
     sl_chain[me] = slope_ref[...]
     got_ref[me] = send_ref[me]
-    pl.when(core == 0)(lambda: relay(0, 1))
-
-    @pl.when(core == 1)
-    def _():
-        pl.when(along_x(1) != 1)(lambda: relay(0, 3))
-        pl.when(along_x(1) == 1)(lambda: relay(1, 3))
-
-    pl.when(me == 1)(lambda: send_own(0))
-    pl.when((me != 0) & (me != 1))(lambda: send_own(1))
+    first_relays()
+    second_sends()
     for r in range(1, nc):
         element_copy(me, lax.rem(me + r, nc)).wait_recv()
-
-    cap = got_ref.shape[2]
-    ed = (got_ref.shape[1] - 8) // 2
-    block = spread_ref.shape[0]
-    lines = 128
-    base = lax.broadcasted_iota(jnp.int32, (lines, cap), 0)
-    variable = lax.broadcasted_iota(jnp.int32, (nvars, cap), 0)
-    matches = [(variable == got_ref[s, 2 * ed : 2 * ed + 1, :].astype(jnp.int32)).astype(F32).astype(BF16) for s in range(nc)]
-    matches = jnp.concatenate(matches + matches, axis=1)
-
-    def rhs_copy(to, source):
-        return remote(rpart.at[at_group(to), :], rbuf.at[source], r_send.at[to], r_recv.at[source], to, band)
-
-    def rhs_part_copy(to, n):
-        at = pl.ds(pl.multiple_of(n * block, block), block)
-        return remote(rpart.at[at_group(to), at], rbuf.at[0, :, at], rp_send.at[to, n], rp_recv.at[n], to, band)
-
-    def send_rhs():
-        for r in range(1, nc):
-            rhs_copy(lax.rem(me + r, nc), me).start()
-
-    def rhs_wait(k):
-        pl.when(k != me)(lambda: rhs_copy(me, k).wait_recv())
-
-    def one_block(n, carry):
-        def one_source(s, inner):
-            values = got_ref[s, 0:ed, :]
-            dofs = got_ref[s, ed : 2 * ed, :].astype(jnp.int32) - n * block
-            for half in range(block // lines):
-                total = jnp.zeros((lines, cap), F32)
-                for i in range(ed):
-                    hit = base == dofs[i : i + 1, :] - half * lines
-                    total = jnp.where(hit, values[i : i + 1, :], total)
-                high = total.astype(BF16)
-                at = pl.ds(pl.multiple_of(s * cap, cap), cap)
-                spread_ref[half * lines : (half + 1) * lines, at] = high
-                at = pl.ds(pl.multiple_of((s + nc) * cap, cap), cap)
-                spread_ref[half * lines : (half + 1) * lines, at] = (total - high.astype(F32)).astype(BF16)
-            return inner
-
-        lax.fori_loop(0, nc, one_source, 0)
-        at = pl.ds(pl.multiple_of(n * block, block), block)
-        rpart[:, at] = lax.dot_general(matches, spread_ref[...], nt, preferred_element_type=F32)
-
-        @pl.when(me == 0)
-        def _():
-            for r in range(1, nc):
-                rhs_part_copy(r, n).start()
-
-        return carry
-
-    lax.fori_loop(0, width // block, one_block, 0)
-
-    rbuf[me] = rpart[at_group(me), :]
 
     for r in range(1, nc):
         slope_chain_copy(me, lax.rem(me + r, nc)).wait_recv()
@@ -332,7 +306,7 @@
         slope_band_copy(r).start()
 
     def slope_term():
-        for r in range(1, nb):
+        for r in others:
             slope_band_arrival(r).wait_recv()
         total = sl_band[0]
         for b in range(1, nb):
@@ -348,19 +322,74 @@
             mass_terms = jnp.where(line < 3, high, jnp.where(line < 5, middle, jnp.where(line == 5, low, 0.0)))
             outer[k] = lax.dot_general(slope_terms.astype(BF16), mass_terms.astype(BF16), (((0,), (0,)), ((), ())), preferred_element_type=F32)
 
-    @pl.when(core == 0)
-    def _():
-        relay(1, 1)
-        relay(0, 3)
-        relay(1, 3)
-
-    @pl.when(core == 1)
-    def _():
-        pl.when(along_x(1) != 1)(lambda: relay(1, 3))
-        pl.when(along_x(1) == 1)(lambda: relay(0, 3))
-        relay(0, 1)
-        relay(1, 1)
-
+    cap = got_ref.shape[2]
+    ed = (got_ref.shape[1] - 8) // 2
+    block = spread_ref.shape[0]
+    lines = 256
+    base = lax.broadcasted_iota(jnp.int32, (lines, cap), 0).astype(F32).astype(BF16)
+    variable = lax.broadcasted_iota(jnp.int32, (nvars, cap), 0)
+    matches = [(variable == got_ref[s, 2 * ed : 2 * ed + 1, :].astype(jnp.int32)).astype(F32).astype(BF16) for s in range(nc)]
+    matches = jnp.concatenate(matches + matches, axis=1)
+
+    def band_copy(to, source):
+        return remote(rpart.at[:, at_band(to)], rslots.at[source], rq_send.at[to], rq_recv.at[source], me, to)
+
+    per_block = block // cols
+
+    def one_block(step, carry):
+        n = lax.rem(step + 1 + band // per_block, width // block)
+
+        def one_source(s, inner):
+            values = got_ref[s, 0:ed, :]
+            high = values.astype(BF16)
+            low = (values - high.astype(F32)).astype(BF16)
+            dofs = got_ref[s, ed : 2 * ed, :].astype(jnp.int32) - n * block
+            for part_no in range(block // lines):
+                shifted = dofs - part_no * lines
+                shifted = jnp.where((shifted >= 0) & (shifted < lines), shifted, -1)
+                place = shifted.astype(F32).astype(BF16)
+                total_high = jnp.zeros((lines, cap), BF16)
+                total_low = jnp.zeros((lines, cap), BF16)
+                for i in range(ed):
+                    hit = base == place[i : i + 1, :]
+                    total_high = jnp.where(hit, high[i : i + 1, :], total_high)
+                    total_low = jnp.where(hit, low[i : i + 1, :], total_low)
+                at = pl.ds(pl.multiple_of(s * cap, cap), cap)
+                spread_ref[part_no * lines : (part_no + 1) * lines, at] = total_high
+                at = pl.ds(pl.multiple_of((s + nc) * cap, cap), cap)
+                spread_ref[part_no * lines : (part_no + 1) * lines, at] = total_low
+            return inner
+
+        lax.fori_loop(0, nc, one_source, 0)
+        at = pl.ds(pl.multiple_of(n * block, block), block)
+        rpart[:, at] = lax.dot_general(matches, spread_ref[...], nt, preferred_element_type=F32)
+
+        for j in range(per_block):
+            to = n * per_block + j
+            pl.when(to != band)(lambda to=to: band_copy(to, band).start())
+
+        return carry
+
+    lax.fori_loop(0, width // block, one_block, 0)
+
+    slope_term()
+    total = rpart[:, at_band(band)]
+    for r in others:
+        band_copy(band, band_from(r)).wait_recv()
+        total = total + rslots[band_from(r)]
+    rsum[...] = total
+
+    def rhs_copy(to, source):
+        return remote(rsum.at[at_group(to), :], rpiece.at[source], r_send.at[to], r_recv.at[source], to, band)
+
+    for r in range(1, nc):
+        rhs_copy(lax.rem(me + r, nc), me).start()
+    rpiece[me] = rsum[at_group(me), :]
+
+    def rhs_wait(k):
+        pl.when(k != me)(lambda: rhs_copy(me, k).wait_recv())
+
+    second_relays()
 
     def rs_copy(r):
         to = band_to(r)
@@ -430,42 +459,33 @@
         wide = lax.dot_general(both, weights, dims, preferred_element_type=F32)
         return wide[:rows] + wide[rows:]
 
-    @pl.when(me != 0)
-    def _():
-        for n in range(width // block):
-            rhs_part_copy(me, n).wait_recv()
-
-    part[...] = rbuf[0]
-    pl.when(me == 1)(send_rhs)
+    rhs_wait(0)
+    gather_start(rpiece[0] + outer[0, at_group(me), :])
+    relay_farthest(0, 0)
+    relay_farthest(1, 1)
+    relay_farthest(0, 1)
+    split_diag(0)
 
     def forward(k, carry):
-        reduce_start()
-        pl.when(me == k + 2)(send_rhs)
-        pl.when(k > 0)(gather_sent)
-        pl.when(k == 0)(lambda: relay_farthest(0, 0))
-        pl.when(k == 0)(slope_term)
-        relay_farthest(0, k + 1)
-        relay_farthest(1, k + 1)
-        split_diag(k)
-        gather_start(reduce_end(part[:, at_band(band)] + outer[k, at_group(me), :]))
-        reduce_sent()
-
-        @pl.when(k + 1 < nc)
-        def _():
-            split_coup(k + 1)
-
+        pl.when(k > 0)(reduce_sent)
+        split_coup(k + 1)
         gather_end()
         solved = narrow(full[...], dsplit[k], nt)
+        part[...] = -spread(solved, csplit[k + 1], nt)
+        reduce_start()
         ybuf[k] = solved
-
-        @pl.when(k + 1 < nc)
-        def _():
-            rhs_wait(k + 1)
-            part[...] = rbuf[k + 1] - spread(solved, csplit[k + 1], nt)
-
+        gather_sent()
+        rhs_wait(k + 1)
+        relay_farthest(1, k + 2)
+        relay_farthest(0, k + 2)
+        split_diag(k + 1)
+        gather_start(reduce_end(part[:, at_band(band)] + (rpiece[k + 1] + outer[k + 1, at_group(me), :])))
         return carry
 
-    lax.fori_loop(0, nc, forward, 0)
+    lax.fori_loop(0, nc - 1, forward, 0)
+    reduce_sent()
+    gather_end()
+    ybuf[nc - 1] = narrow(full[...], dsplit[nc - 1], nt)
 
     def out_copy(k, source):
         return remote(xbuf.at[k], out_ref.at[at_group(source), :], out_send.at[k], out_recv.at[source], k, band)
@@ -507,13 +527,7 @@
         other = lax.rem(me + r, nc)
         out_copy(other, me).wait_send()
         out_copy(me, other).wait_recv()
-        pl.when(me != 0)(lambda other=other: rhs_copy(other, me).wait_send())
-
-        @pl.when(me == 0)
-        def _():
-            for n in range(width // block):
-                rhs_part_copy(other, n).wait_send()
-
+        rhs_copy(other, me).wait_send()
         slope_chain_copy(other, me).wait_send()
         mode_chain_copy(other, me).wait_send()
         element_copy(other, me).wait_send()
@@ -521,6 +535,7 @@
     for r in range(1, nb):
         slope_band_copy(r).wait_send()
         mode_band_copy(r).wait_send()
+        band_copy(band_to(r), band).wait_send()
 
     def sent(which):
         for i in range(3):
@@ -552,9 +567,14 @@
     eigvec_slope, eigval_slope = pl.pallas_call(
         functools.partial(solve_kernel, nc, nb),
         out_shape=(jax.ShapeDtypeStruct((VARS, cols), F32), jax.ShapeDtypeStruct((1, VARS), F32)),
-        in_specs=[pl.BlockSpec(memory_space=pltpu.SMEM)] + [anywhere] * 4 + [vmem] * 5,
+        in_specs=[pl.BlockSpec(memory_space=pltpu.SMEM)] + [anywhere] * 9,
         out_specs=(vmem, vmem),
         scratch_shapes=[
+            pltpu.VMEM((ed, count), jnp.int32),
+            pltpu.VMEM((1, count), jnp.int32),
+            pltpu.VMEM((1, count), jnp.int32),
+            pltpu.VMEM((1, cols), F32),
+            pltpu.VMEM((1, cols), F32),
             pltpu.VMEM((ed, ed, count), F32),
             pltpu.VMEM((ed, ed, count), F32),
             pltpu.VMEM((8, cols), F32),
@@ -572,7 +592,9 @@
             pltpu.VMEM((nc, width, 2 * cols), BF16),
             pltpu.VMEM((256, 2 * nc * cap), BF16),
             pltpu.VMEM((VARS, width), F32),
-            pltpu.VMEM((nc, rows, width), F32),
+            pltpu.VMEM((nb, VARS, cols), F32),
+            pltpu.VMEM((VARS, cols), F32),
+            pltpu.VMEM((nc, rows, cols), F32),
             pltpu.VMEM((nc, 8, padded), F32),
             pltpu.VMEM((nb, 8, padded), F32),
             pltpu.VMEM((nc, padded, cols), F32),
@@ -582,10 +604,10 @@
             pltpu.VMEM((rows, width), F32),
             pltpu.VMEM((nc, rows, cols), F32),
             pltpu.VMEM((nc, rows, cols), F32),
-            dma((2,)), dma((nc,)), dma((nc,)), dma((nb,)), dma((nb,)), dma((nc,)), dma((nc,)),
+            dma((7,)), dma((nc,)), dma((nc,)), dma((nb,)), dma((nb,)), dma((nc,)), dma((nc,)),
             dma((2, nc)), dma((2, 3)), dma((2, 4, 2)),
             dma((nc,)), dma((nc,)), dma((nb,)), dma((nb,)), dma((nc,)), dma((nc,)),
-            dma((nc, 8)), dma((8,)),
+            dma((nb,)), dma((nb,)),
             dma((nb,)), dma((nb,)), dma((nb,)), dma((nb,)), dma((nc,)), dma((nc,)),
         ],
         compiler_params=pltpu.CompilerParams(collective_id=0, has_side_effects=True, vmem_limit_bytes=52 * 1024 * 1024),

time: 264 us -> 256 us (0.970)
  Pallas kernels: 257 us -> 249 us
    pallas_call x1, Pallas kernels: 257 us -> 249 us  [on_device(): pl.pallas_call(functools.partial(solve_kernel, nc, nb), out_shape=(jax.Sh...]
where the time goes in v5:
time: 256 us
  Pallas kernels  249 us (97%)
  local copies, waits for them, and re-layouts  5.36 us (2%)
    pallas_call x1, Pallas kernels, on_device(): pl.pallas_call(functools.partial(solve_kernel, nc, nb), out_shape=(jax.Sh...  249 us
    unnamed x14, local copies, waits for them, and re-layouts  5.28 us

profile of v5, /device:TPU:0, one launch (start us, length us, event | category | flops | bytes accessed | tf_op | source)
XLA Modules:
  0.0 255.6 jit_solution(3974249348691985916)
XLA Ops:
  0.6 0.0 copy-start
  1.3 0.0 copy-done
  1.3 0.1 dynamic-slice_bitcast_fusion.mass_in
  1.4 0.0 copy-start.1
  1.4 1.2 copy-done.1
  2.6 0.0 copy-start.2
  2.6 0.8 copy-done.2
  3.4 0.0 copy-start.3
  3.4 0.7 copy-done.3
  4.1 0.0 copy-start.4
  4.1 0.7 copy-done.4
  4.8 0.0 copy-start.5
  4.8 0.7 copy-done.5
  5.5 248.9 %solve.1 = (f32[192,128]{1,0:T(8,128)S(1)}, f32[1,192]{1,0:T(1,128)S(1)}) custom-call(f32[1]{0:T(128)S(6)} %copy.14.lam_ref, f32[128,2048]{1,0:T(8,128)S(1)} %copy-done.1, f32[2048,128]{1,0:T(8,128)} %coup_ref.1, f32[24,24,512]{2,1,0:T(8,128)} %stiff_ref.1, f32[24,24,512]{2,1,0:T(8,128)} %emass_ref.1, s32[24,512]{1,0:T(8,128)S(1)} %copy-done.2, ...), custom_call_target="tpu_custom_call" | custom-call | flops 10000000000 | bytes 100000000 | tf_op jit(solution)/shard_map/solve/pallas_call | solution.py:567
  254.4 0.6 copy.15
  255.0 0.6 copy.16
Async XLA Ops:
  0.6 0.7 copy-start
  1.4 1.2 copy-start.1
  2.6 0.8 copy-start.2
  3.4 0.7 copy-start.3
  4.1 0.7 copy-start.4
  4.8 0.7 copy-start.5

commit v6 on v5

--- a/solution.py
+++ b/solution.py
@@ -111,7 +111,7 @@
 
     side = math.isqrt(nb)
     hops = lambda r: min(r // side, side - r // side) + min(r % side, side - r % side)
-    others = sorted(range(1, nb), key=lambda r: (-hops(r), r))
+    others = sorted(range(1, nb), key=lambda r: (-hops(r), (r * 7) % 16))
     band_z, band_y = band // side, lax.rem(band, side)
 
     def band_to(r):

time: 256 us -> 254 us (level)
  no operation moved by 1% of the time
where the time goes in v6:
time: 254 us
  Pallas kernels  247 us (97%)
  local copies, waits for them, and re-layouts  5.36 us (2%)
    pallas_call x1, Pallas kernels, on_device(): pl.pallas_call(functools.partial(solve_kernel, nc, nb), out_shape=(jax.Sh...  247 us
    unnamed x14, local copies, waits for them, and re-layouts  5.28 us

profile of v6, /device:TPU:0, one launch (start us, length us, event | category | flops | bytes accessed | tf_op | source)
XLA Modules:
  0.0 253.9 jit_solution(4908710932912794305)
XLA Ops:
  0.6 0.0 copy-start
  1.3 0.0 copy-done
  1.3 0.1 dynamic-slice_bitcast_fusion.mass_in
  1.4 0.0 copy-start.1
  1.4 1.2 copy-done.1
  2.6 0.0 copy-start.2
  2.6 0.8 copy-done.2
  3.4 0.0 copy-start.3
  3.4 0.7 copy-done.3
  4.1 0.0 copy-start.4
  4.1 0.7 copy-done.4
  4.8 0.0 copy-start.5
  4.8 0.7 copy-done.5
  5.5 247.3 %solve.1 = (f32[192,128]{1,0:T(8,128)S(1)}, f32[1,192]{1,0:T(1,128)S(1)}) custom-call(f32[1]{0:T(128)S(6)} %copy.14.lam_ref, f32[128,2048]{1,0:T(8,128)S(1)} %copy-done.1, f32[2048,128]{1,0:T(8,128)} %coup_ref.1, f32[24,24,512]{2,1,0:T(8,128)} %stiff_ref.1, f32[24,24,512]{2,1,0:T(8,128)} %emass_ref.1, s32[24,512]{1,0:T(8,128)S(1)} %copy-done.2, ...), custom_call_target="tpu_custom_call" | custom-call | flops 10000000000 | bytes 100000000 | tf_op jit(solution)/shard_map/solve/pallas_call | solution.py:567
  252.7 0.6 copy.15
  253.4 0.6 copy.16
Async XLA Ops:
  0.6 0.7 copy-start
  1.4 1.2 copy-start.1
  2.6 0.8 copy-start.2
  3.4 0.7 copy-start.3
  4.1 0.7 copy-start.4
  4.8 0.7 copy-start.5

commit v7 on v6

--- a/solution.py
+++ b/solution.py
@@ -114,11 +114,9 @@
     others = sorted(range(1, nb), key=lambda r: (-hops(r), (r * 7) % 16))
     band_z, band_y = band // side, lax.rem(band, side)
 
-    def band_to(r):
-        return lax.rem(band_z + r // side, side) * side + lax.rem(band_y + r % side, side)
-
-    def band_from(r):
-        return lax.rem(band_z + side - r // side, side) * side + lax.rem(band_y + side - r % side, side)
+    towards = {r: lax.rem(band_z + r // side, side) * side + lax.rem(band_y + r % side, side) for r in others}
+    behind = {r: lax.rem(band_z + side - r // side, side) * side + lax.rem(band_y + side - r % side, side) for r in others}
+    band_to, band_from = towards.__getitem__, behind.__getitem__
 
     def at_group(c):
         return pl.ds(pl.multiple_of(c * rows, 8), rows)
@@ -325,7 +323,7 @@
     cap = got_ref.shape[2]
     ed = (got_ref.shape[1] - 8) // 2
     block = spread_ref.shape[0]
-    lines = 256
+    lines = 128
     base = lax.broadcasted_iota(jnp.int32, (lines, cap), 0).astype(F32).astype(BF16)
     variable = lax.broadcasted_iota(jnp.int32, (nvars, cap), 0)
     matches = [(variable == got_ref[s, 2 * ed : 2 * ed + 1, :].astype(jnp.int32)).astype(F32).astype(BF16) for s in range(nc)]

time: 254 us -> 254 us (level)
  no operation moved by 1% of the time
where the time goes in v7:
time: 254 us
  Pallas kernels  247 us (97%)
  local copies, waits for them, and re-layouts  5.36 us (2%)
    pallas_call x1, Pallas kernels, on_device(): pl.pallas_call(functools.partial(solve_kernel, nc, nb), out_shape=(jax.Sh...  247 us
    unnamed x14, local copies, waits for them, and re-layouts  5.28 us

profile of v7, /device:TPU:0, one launch (start us, length us, event | category | flops | bytes accessed | tf_op | source)
XLA Modules:
  0.0 253.6 jit_solution(3476220169175886899)
XLA Ops:
  0.6 0.0 copy-start
  1.3 0.0 copy-done
  1.3 0.1 dynamic-slice_bitcast_fusion.mass_in
  1.4 0.0 copy-start.1
  1.4 1.2 copy-done.1
  2.6 0.0 copy-start.2
  2.6 0.8 copy-done.2
  3.4 0.0 copy-start.3
  3.4 0.7 copy-done.3
  4.1 0.0 copy-start.4
  4.1 0.7 copy-done.4
  4.8 0.0 copy-start.5
  4.8 0.7 copy-done.5
  5.5 246.9 %solve.1 = (f32[192,128]{1,0:T(8,128)S(1)}, f32[1,192]{1,0:T(1,128)S(1)}) custom-call(f32[1]{0:T(128)S(6)} %copy.14.lam_ref, f32[128,2048]{1,0:T(8,128)S(1)} %copy-done.1, f32[2048,128]{1,0:T(8,128)} %coup_ref.1, f32[24,24,512]{2,1,0:T(8,128)} %stiff_ref.1, f32[24,24,512]{2,1,0:T(8,128)} %emass_ref.1, s32[24,512]{1,0:T(8,128)S(1)} %copy-done.2, ...), custom_call_target="tpu_custom_call" | custom-call | flops 10000000000 | bytes 100000000 | tf_op jit(solution)/shard_map/solve/pallas_call | solution.py:565
  252.4 0.6 copy.15
  253.0 0.6 copy.16
Async XLA Ops:
  0.6 0.7 copy-start
  1.4 1.2 copy-start.1
  2.6 0.8 copy-start.2
  3.4 0.7 copy-start.3
  4.1 0.7 copy-start.4
  4.8 0.7 copy-start.5
